TPU v7x, 32 devices: a whole 2x2x4 slice. The times are simulated.
32 devices in a mesh: tok: 16 (over z, y, x), ch: 2 (over core).
Axes of the slice: x: 2, y: 2, z: 4, core: 2. Of those that a mesh axis runs over, the one named last changes fastest.
Arguments:
- fields: float32 [16384, 1024], P('tok', 'ch'), may hold values from -20 to 20
- gain_one: float32 [1024], P('ch'), may hold values from 0.1 to 1.9
- tok_in_weight: float32 [3072, 16384], P('ch', 'tok'), may hold values from -0.046875 to 0.046875
- tok_in_bias: float32 [3072], P('ch'), may hold values from -3 to 3
- tok_out_weight: float32 [16384, 3072], P('tok', 'ch'), may hold values from -0.109375 to 0.109375
- gain_two: float32 [1024], P('ch'), may hold values from 0.1 to 1.9
- ch_in_weight: float32 [1024, 6144], P('tok', 'ch'), may hold values from -0.1875 to 0.1875
- ch_in_bias: float32 [6144], P('ch'), may hold values from -3 to 3
- ch_out_weight: float32 [6144, 1024], P('ch', 'tok'), may hold values from -0.078125 to 0.078125
Outputs:
- block_out: float32 [16384, 1024], P('tok', 'ch')
All inputs are finite; a program needn't handle non-finite values.
Results may differ from a plain program's by a relative error of at most 0.000086.
Values sent between devices are 32-bit elements; how exact they have to be, the bound alone decides.
No kernel may reach another device: no remote copies, remote signals or barrier semaphores. Data moves between devices by JAX's collectives and lax.ppermute only.
A program may use at most 128 MiB of HBM per device.

v0:
```python
import jax
import jax.numpy as jnp
from jax import lax
from jax.sharding import PartitionSpec as P

epsilon = 1e-05
highest = lax.Precision.HIGHEST


def matmul(left, right):
    return jnp.dot(left, right, precision=highest, preferred_element_type=jnp.float32)


def local_norm(values, gain):
    centre = jnp.mean(values, axis=1, keepdims=True)
    centred = values - centre
    spread = jnp.mean(centred * centred, axis=1, keepdims=True)
    return centred * lax.rsqrt(spread + epsilon) * gain


def shards(
    fields,
    gain_one,
    tok_in_weight,
    tok_in_bias,
    tok_out_weight,
    gain_two,
    ch_in_weight,
    ch_in_bias,
    ch_out_weight,
):
    ch_place = lax.axis_index("ch")
    tok_rows, ch_width = fields.shape
    full_fields, full_gain_one, full_gain_two = (
        lax.all_gather(fields, "ch", axis=1, tiled=True),
        lax.all_gather(gain_one, "ch", axis=0, tiled=True),
        lax.all_gather(gain_two, "ch", axis=0, tiled=True),
    )
    normed = local_norm(full_fields, full_gain_one)
    columns = normed
    summed_cols = lax.psum_scatter(
        lax.dot_general(
            columns,
            tok_in_weight,
            (((0,), (1,)), ((), ())),
            precision=highest,
            preferred_element_type=jnp.float32,
        ),
        "tok",
        scatter_dimension=0,
        tiled=True,
    )
    activated = jax.nn.gelu(summed_cols + tok_in_bias[None, :], approximate=False)
    partial_value = lax.dot_general(
        tok_out_weight,
        lax.all_gather(activated, "tok", axis=0, tiled=True),
        (((1,), (1,)), ((), ())),
        precision=highest,
        preferred_element_type=jnp.float32,
    )
    mixed_sum = lax.psum(partial_value, "ch")
    updated = full_fields + mixed_sum
    normed_two = local_norm(updated, full_gain_two)
    kept_rows = lax.dynamic_slice_in_dim(updated, ch_place * ch_width, ch_width, 1)
    columns = normed_two
    hidden_sum = matmul(columns, lax.all_gather(ch_in_weight, "tok", axis=0, tiled=True))
    activated_two = jax.nn.gelu(hidden_sum + ch_in_bias[None, :], approximate=False)
    channel_terms = matmul(activated_two, lax.all_gather(ch_out_weight, "tok", axis=1, tiled=True))
    return kept_rows + lax.psum_scatter(channel_terms, "ch", scatter_dimension=1, tiled=True)


def solution(mesh):
    in_specs = (
        P("tok", "ch"),
        P("ch"),
        P("ch", "tok"),
        P("ch"),
        P("tok", "ch"),
        P("ch"),
        P("tok", "ch"),
        P("ch"),
        P("ch", "tok"),
    )
    out_specs = P("tok", "ch")
    return jax.shard_map(shards, mesh=mesh, in_specs=in_specs, out_specs=out_specs, check_vma=False)
```

profile of v0, /device:TPU:0, one launch (start us, length us, event | category | flops | bytes accessed | tf_op | source)
XLA Modules:
  0.0 757.1 jit_solution(3616305652247287986)
XLA Ops:
  6.5 2.9 copy.13
  9.4 0.0 all-gather.7.cloned.1.call-update
  9.4 0.0 reduce-scatter.3.cloned.1.call-start
  9.5 2.1 all-gather
  11.6 14.4 %all-gather.7.cloned.1.call-done = f32[1024,1024]{0,1:T(8,128)} async-done(((f32[1024,512]{0,1:T(8,128)}), f32[1024,1024]{0,1:T(8,128)}) %all-gather.7.cloned.1.call-update) | async-done | bytes 4194320 | tf_op jit(solution)/shard_map/all_gather | solution.py:35
  26.0 2.5 reduce_sum.36
  28.4 2.7 multiply_reduce_fusion.1
  31.1 25.2 %fusion.94 = f32[1024,1536]{1,0:T(8,128)} fusion(f32[1536,1024]{1,0:T(8,128)} %param.11, f32[1024,1024]{0,1:T(8,128)} %all-gather.7.cloned.1.call-done, f32[1024]{0:T(1024)S(1)} %bitcast.13, f32[1024]{0:T(1024)S(1)} %add_rsqrt_fusion.1, f32[1024]{0:T(1024)S(1)} %broadcast_multiply_fusion.1), kind=kOutput, calls=%fused_computation.100 | convolution fusion | flops 19330498560 | bytes 16789504 | tf_op jit(solution)/shard_map/dot_general | solution.py:42
  56.3 0.0 reduce-scatter.3.cloned.1.call-update
  56.4 0.0 all-gather.9.cloned.1.call-start
  56.4 147.1 %reduce-scatter.3.cloned.1.call-done = f32[64,1536]{1,0:T(8,128)} async-done(((f32[1024,1536]{1,0:T(8,128)}), f32[64,1536]{1,0:T(8,128)}) %reduce-scatter.3.cloned.1.call-update) | async-done | bytes 393232 | tf_op jit(solution)/shard_map/reduce_scatter | solution.py:41
  203.5 2.6 fusion.106
  206.1 0.0 all-reduce.2.cloned.1.call-start
  206.1 93.4 %all-gather.9.cloned.1.call-done = f32[1024,1536]{1,0:T(8,128)} async-done(((f32[64,1536]{1,0:T(8,128)}), f32[1024,1536]{1,0:T(8,128)}) %all-gather.9.cloned.1.call-update) | async-done | bytes 6291472 | tf_op jit(solution)/shard_map/all_gather | solution.py:56
  299.6 24.7 %convolution_bitcast_fusion = f32[1024,1024]{0,1:T(8,128)} fusion(f32[1024,1536]{1,0:T(8,128)} %all-gather.9.cloned.1.call-done, f32[1024,1536]{1,0:T(8,128)} %param.13), kind=kOutput, calls=%fused_computation.106 | convolution fusion | flops 19327352832 | bytes 16777216 | tf_op jit(solution)/shard_map/dot_general | solution.py:54
  324.3 0.0 all-gather.11.cloned.1.call-start
  324.3 0.5 all-gather.11.cloned.1.call-update
  324.9 0.0 all-gather.13.cloned.1.call-start
  324.9 0.5 all-gather.13.cloned.1.call-update
  325.4 0.0 reduce-scatter.5.cloned.1.call-start
  325.5 2.0 all-gather.1
  327.4 23.7 %all-reduce.2.cloned.1.call-done = f32[1024,1024]{0,1:T(8,128)} async-done(((f32[1024,1024]{0,1:T(8,128)}), f32[1024,1024]{0,1:T(8,128)}) %all-reduce.2.cloned.1.call-update) | async-done | bytes 4194320 | tf_op jit(solution)/shard_map/psum | solution.py:61
  351.1 4.5 fusion.144
  355.6 1.9 copy-done
  357.6 0.5 multiply_reduce_fusion
  358.1 149.3 %all-gather.11.cloned.1.call-done = f32[1024,3072]{1,0:T(8,128)} async-done(((f32[64,3072]{1,0:T(8,128)}), f32[1024,3072]{1,0:T(8,128)}) %all-gather.11.cloned.1.call-update) | async-done | bytes 12582928 | tf_op jit(solution)/shard_map/all_gather | solution.py:66
  507.4 48.0 %fusion.91 = f32[1024,3072]{1,0:T(8,128)} fusion(f32[1024,3072]{1,0:T(8,128)} %all-gather.11.cloned.1.call-done, f32[1024,1024]{0,1:T(8,128)} %copy-done, f32[1024]{0:T(1024)S(1)} %bitcast.12, f32[1024]{0:T(1024)S(1)} %add_rsqrt_fusion, f32[1024]{0:T(1024)S(1)} %broadcast_multiply_fusion), kind=kOutput, calls=%fused_computation.96 | convolution fusion | flops 38657851392 | bytes 29372416 | tf_op jit(solution)/shard_map/dot_general | solution.py:11
  555.3 105.3 %all-gather.13.cloned.1.call-done = f32[3072,1024]{0,1:T(8,128)} async-done(((f32[3072,64]{0,1:T(8,128)}), f32[3072,1024]{0,1:T(8,128)}) %all-gather.13.cloned.1.call-update) | async-done | bytes 12582928 | tf_op jit(solution)/shard_map/all_gather | solution.py:68
  660.6 74.8 %fusion.2 = f32[1024,1024]{0,1:T(8,128)} fusion(f32[3072,1024]{0,1:T(8,128)} %all-gather.13.cloned.1.call-done, f32[1024,3072]{1,0:T(8,128)} %fusion.91, f32[3072]{0:T(1024)S(1)} %copy-done.3), kind=kOutput, calls=%fused_computation.3 | convolution fusion | flops 38859177984 | bytes 29372416 | tf_op jit(solution)/shard_map/dot_general | solution.py:11
  735.5 10.4 %reduce-scatter.5.cloned.1.call-done = f32[1024,512]{0,1:T(8,128)} async-done(((f32[1024,1024]{0,1:T(8,128)}), f32[1024,512]{0,1:T(8,128)}) %reduce-scatter.5.cloned.1.call-update) | async-done | bytes 2097168 | tf_op jit(solution)/shard_map/reduce_scatter | solution.py:69
  745.8 2.6 dynamic-slice_add_fusion
  748.4 1.8 copy.15
  (15 shorter events, 0.1 us)
Async XLA Ops:
  6.5 19.4 %all-gather.7.cloned.1.call-start = ((), (), s32[]{:S(2)}) async-start(), calls=%async_computation.2 | async-start | bytes 6291456 | tf_op jit(solution)/shard_map/all_gather | solution.py:35
  9.4 194.0 %reduce-scatter.3.cloned.1.call-start = ((), (), s32[]{:S(2)}) async-start(), calls=%async_computation.3 | async-start | bytes 6684672 | tf_op jit(solution)/shard_map/reduce_scatter | solution.py:41
  31.1 172.3 %copy-start.1 = (f32[1536]{0:T(1024)S(1)}, f32[1536]{0:T(1024)}, u32[]{:S(2)}) copy-start(f32[1536]{0:T(1024)} %param.12) | copy-start | bytes 18436
  56.4 243.2 %all-gather.9.cloned.1.call-start = ((), (), s32[]{:S(2)}) async-start(), calls=%async_computation.4 | async-start | bytes 6684672 | tf_op jit(solution)/shard_map/all_gather | solution.py:56
  206.1 119.4 %copy-start.2 = (f32[512]{0:T(512)S(1)}, f32[512]{0:T(512)}, u32[]{:S(2)}) copy-start(f32[512]{0:T(512)} %param.14) | copy-start | bytes 6148
  206.1 145.0 %all-reduce.2.cloned.1.call-start = ((), (), s32[]{:S(2)}) async-start(), calls=%async_computation.5 | async-start | bytes 8388608 | tf_op jit(solution)/shard_map/psum | solution.py:61
  324.3 183.1 %all-gather.11.cloned.1.call-start = ((), (), s32[]{:S(2)}) async-start(), calls=%async_computation.6 | async-start | bytes 13369344 | tf_op jit(solution)/shard_map/all_gather | solution.py:66
  324.9 335.8 %all-gather.13.cloned.1.call-start = ((), (), s32[]{:S(2)}) async-start(), calls=%async_computation.7 | async-start | bytes 13369344 | tf_op jit(solution)/shard_map/all_gather | solution.py:68
  325.4 420.4 %reduce-scatter.5.cloned.1.call-start = ((), (), s32[]{:S(2)}) async-start(), calls=%async_computation.8 | async-start | bytes 6291456 | tf_op jit(solution)/shard_map/reduce_scatter | solution.py:69
  355.6 2.0 copy-start
  507.4 153.2 %copy-start.3 = (f32[3072]{0:T(1024)S(1)}, f32[3072]{0:T(1024)}, u32[]{:S(2)}) copy-start(f32[3072]{0:T(1024)} %param.16) | copy-start | bytes 36868
Sparse Core Ops, SparseCore 0:
  9.6 16.3 all-gather.6
  56.5 146.9 reduce-scatter.2
  206.2 93.2 all-gather.8
  324.4 26.7 all-reduce.1
  354.1 153.1 all-gather.10
  510.4 150.1 all-gather.12
  735.6 10.2 reduce-scatter.4
where the time goes:
time: 757 us
  waiting for transfers between devices  545 us (72%)
  matrix products  173 us (23%)
  other arithmetic  15.3 us (2%)
  between operations  13.5 us (2%)
    all_gather x1, waiting for transfers between devices, shards(): lax.all_gather(ch_in_weight, 'tok', axis=0, tiled=True)  149 us
    reduce_scatter x1, waiting for transfers between devices, shards(): lax.psum_scatter(lax.dot_general(columns, tok_in_weight, (((0,), (1,)), (...  147 us
    dot_general x2, matrix products, matmul(): jnp.dot(left, right, precision=highest, preferred_element_type=jnp.float32)  123 us
    all_gather x1, waiting for transfers between devices, shards(): lax.all_gather(ch_out_weight, 'tok', axis=1, tiled=True)  105 us
    all_gather x1, waiting for transfers between devices, shards(): lax.all_gather(activated, 'tok', axis=0, tiled=True)  93.4 us
    dot_general x1, matrix products, shards(): lax.dot_general(columns, tok_in_weight, (((0,), (1,)), ((), ())), precisi...  25.2 us
    dot_general x1, matrix products, shards(): lax.dot_general(tok_out_weight, lax.all_gather(activated, 'tok', axis=0,...  24.7 us
    psum x1, waiting for transfers between devices, shards(): mixed_sum = lax.psum(partial_value, 'ch')  23.7 us
  transfers between devices with their start and end apart: 7, of which 7 were waited for; matrix products, arithmetic and copies ran while one was open for 7% of the time, Pallas kernels for 0%

commit v1 on v0

v1 whole, which is shorter than its diff:
```python
import jax
import jax.numpy as jnp
from jax import lax
from jax.sharding import PartitionSpec as P

epsilon = 1e-05
exact = lax.Precision.HIGH


def contract(left, right, left_dim, right_dim):
    return lax.dot_general(
        left,
        right,
        (((left_dim,), (right_dim,)), ((), ())),
        precision=exact,
        preferred_element_type=jnp.float32,
    )


def column_norm(values, gain):
    centre = jnp.mean(values, axis=0, keepdims=True)
    centred = values - centre
    spread = jnp.mean(centred * centred, axis=0, keepdims=True)
    return centred * lax.rsqrt(spread + epsilon) * gain


class Grid:
    def __init__(self, tok, ch):
        self.tok, self.ch = tok, ch
        self.wide = 2 if tok % 2 == 0 else 1
        self.high = 2 if tok % (2 * self.wide) == 0 else 1
        self.deep = tok // (self.wide * self.high)
        self.sizes = {"z": self.deep, "y": self.high, "x": self.wide}
        self.keys = [(c, b, a) for c in range(self.deep) for b in range(self.high) for a in range(self.wide)]

    def index(self, z, y, x):
        return (z * self.high + y) * self.wide + x

    def place(self):
        me = lax.axis_index("tok")
        return me // (self.high * self.wide), (me // self.wide) % self.high, me % self.wide

    def to_offset(self, value, offset):
        pairs = []
        for z, y, x in self.keys:
            target = (z + offset[0]) % self.deep, (y + offset[1]) % self.high, (x + offset[2]) % self.wide
            pairs.append((self.index(z, y, x), self.index(*target)))
        return lax.ppermute(value, "tok", pairs)

    def to_core(self, value, step):
        return lax.ppermute(value, "ch", [(core, (core + step) % self.ch) for core in range(self.ch)])

    def steps(self, axis):
        position = "zyx".index(axis)
        for step in range(1, self.sizes[axis]):
            yield tuple(step if slot == position else 0 for slot in range(3))

    def minus(self, offset):
        return tuple((-o) % s for o, s in zip(offset, (self.deep, self.high, self.wide)))

    def plus(self, key, offset):
        return tuple((k + o) % s for k, o, s in zip(key, offset, (self.deep, self.high, self.wide)))

    def scatter_sum(self, blocks, order):
        for axis in order:
            position = "zyx".index(axis)
            kept = [key for key in blocks if key[position] == 0]
            arrived = []
            for offset in self.steps(axis):
                sent = jnp.concatenate([blocks[self.plus(key, offset)] for key in kept], axis=0)
                arrived.append(self.to_offset(sent, offset))
            held = jnp.concatenate([blocks[key] for key in kept], axis=0)
            for value in arrived:
                held = held + value
            rows = held.shape[0] // len(kept)
            blocks = {key: held[n * rows : (n + 1) * rows] for n, key in enumerate(kept)}
        return blocks[(0, 0, 0)]

    def gather(self, block, order):
        rows = block.shape[0]
        blocks = {(0, 0, 0): block}
        for axis in order:
            keys = list(blocks)
            held = jnp.concatenate([blocks[key] for key in keys], axis=0)
            for offset in self.steps(axis):
                value = self.to_offset(held, self.minus(offset))
                for n, key in enumerate(keys):
                    blocks[self.plus(key, offset)] = value[n * rows : (n + 1) * rows]
        return jnp.concatenate([blocks[key] for key in self.keys], axis=0)


def cuts(total, parts):
    step = total // parts
    return [(n * step, total if n == parts - 1 else (n + 1) * step) for n in range(parts)]


def shards(
    grid,
    fields,
    gain_one,
    tok_in_weight,
    tok_in_bias,
    tok_out_weight,
    gain_two,
    ch_in_weight,
    ch_in_bias,
    ch_out_weight,
):
    tok, ch = grid.tok, grid.ch
    width = fields.shape[1]
    rows = ch * width // tok
    per_core = width // rows
    core = lax.axis_index("ch")
    z, y, x = grid.place()
    owners = [
        grid.index((z + c) % grid.deep, (y + b) % grid.high, (x + a) % grid.wide) for c, b, a in grid.keys
    ]

    def all_cores(value):
        return jnp.concatenate([value] + [grid.to_core(value, ch - step) for step in range(1, ch)], axis=0)

    def by_offset(value):
        starts = [(((owner // per_core - core) % ch) * per_core + owner % per_core) * rows for owner in owners]
        return jnp.concatenate([lax.dynamic_slice_in_dim(value, start, rows, 0) for start in starts], axis=0)

    def for_core(value, step):
        taken = []
        for n in range(per_core):
            owner = ((core + step) % ch) * per_core + n
            oz, oy, ox = owner // (grid.high * grid.wide), (owner // grid.wide) % grid.high, owner % grid.wide
            start = grid.index((oz - z) % grid.deep, (oy - y) % grid.high, (ox - x) % grid.wide) * rows
            taken.append(lax.dynamic_slice_in_dim(value, start, rows, 0))
        return jnp.concatenate(taken, axis=0)

    full = all_cores(fields.T)
    gains = by_offset(all_cores(gain_one[:, None])), by_offset(all_cores(gain_two[:, None]))
    full = by_offset(full)
    normed = column_norm(full, gains[0])

    hidden = tok_in_weight.shape[0]
    plans = list(zip(cuts(hidden, 3), ("xyz", "yzx", "zxy")))
    activated = []
    for (start, stop), order in plans:
        partial = contract(normed, tok_in_weight[start:stop], 1, 1)
        blocks = {key: partial[n * rows : (n + 1) * rows] for n, key in enumerate(grid.keys)}
        summed = grid.scatter_sum(blocks, order)
        activated.append(jax.nn.gelu(summed + tok_in_bias[None, start:stop], approximate=False))
    mixed_part = 0.0
    for ((start, stop), order), value in zip(plans, activated):
        mixed_part = mixed_part + contract(grid.gather(value, order[::-1]), tok_out_weight[:, start:stop], 1, 1)
    mixed = full + mixed_part
    for step in range(1, ch):
        mixed = mixed + grid.to_core(mixed_part, step)
    normed_two = column_norm(mixed, gains[1])

    first = grid.gather(ch_in_weight, "zxy")
    second = grid.gather(ch_out_weight.T, "yzx")
    hidden_sum = contract(normed_two, first, 0, 0)
    activated_two = jax.nn.gelu(hidden_sum + ch_in_bias[None, :], approximate=False)
    terms = contract(second, activated_two, 1, 1)
    result = for_core(terms + mixed, 0)
    for step in range(1, ch):
        result = result + grid.to_core(for_core(terms, step), step)
    return result.T


def solution(mesh):
    grid = Grid(mesh.shape["tok"], mesh.shape["ch"])
    in_specs = (
        P("tok", "ch"),
        P("ch"),
        P("ch", "tok"),
        P("ch"),
        P("tok", "ch"),
        P("ch"),
        P("tok", "ch"),
        P("ch"),
        P("ch", "tok"),
    )

    def block(*arrays):
        return shards(grid, *arrays)

    return jax.shard_map(block, mesh=mesh, in_specs=in_specs, out_specs=P("tok", "ch"), check_vma=False)
```

time: 757 us -> 716 us (0.946)
  waiting for transfers between devices: 545 us -> 321 us
  starting transfers between devices: 0.25 us -> 191 us
  local copies, waits for them, and re-layouts: 6.64 us -> 72.2 us
  matrix products: 173 us -> 109 us
  between operations: 13.5 us -> 2.69 us
    all_gather x4 -> x0, waiting for transfers between devices: 362 us -> none  [the longest x1 149 us: shards(): lax.all_gather(ch_in_weight, 'tok', axis=0, tiled=True)]
    ppermute x0 -> x45, waiting for transfers between devices: none -> 321 us  [the longest x40 321 us: to_offset(): return lax.ppermute(value, 'tok', pairs)]
    ppermute x0 -> x45, starting transfers between devices: none -> 191 us  [the longest x40 190 us: to_offset(): return lax.ppermute(value, 'tok', pairs)]
    reduce_scatter x2 -> x0, waiting for transfers between devices: 157 us -> none  [the longest x1 147 us: shards(): lax.psum_scatter(lax.dot_general(columns, tok_in_weight, (((0,), (1,)), (...]
    dot_general x4 -> x8, matrix products: 173 us -> 109 us  [contract(): lax.dot_general(left, right, (((left_dim,), (right_dim,)), ((), ())), pre...]
    unnamed x9 -> x136, local copies, waits for them, and re-layouts: 4.83 us -> 62.2 us
    psum x1 -> x0, waiting for transfers between devices: 23.7 us -> none  [shards(): mixed_sum = lax.psum(partial_value, 'ch')]
    concatenate x0 -> x16, local copies, waits for them, and re-layouts: none -> 7.76 us  [the longest x4 3.29 us: gather(): held = jnp.concatenate([blocks[key] for key in keys], axis=0)]
  transfers between devices with their start and end apart: 7 -> 45, of which waited for: 7 -> 19; matrix products, arithmetic and copies ran while one was open for 7% -> 12% of each run, Pallas kernels for 0% -> 0%
where the time goes in v1:
time: 716 us; the launch traced here: 712 us
  waiting for transfers between devices  321 us (45%)
  starting transfers between devices  191 us (27%)
  matrix products  109 us (15%)
  local copies, waits for them, and re-layouts  72.2 us (10%)
  other arithmetic  15.8 us (2%)
    ppermute x40, waiting for transfers between devices, to_offset(): return lax.ppermute(value, 'tok', pairs)  321 us
    ppermute x40, starting transfers between devices, to_offset(): return lax.ppermute(value, 'tok', pairs)  190 us
    dot_general x8, matrix products, contract(): lax.dot_general(left, right, (((left_dim,), (right_dim,)), ((), ())), pre...  109 us
    unnamed x136, local copies, waits for them, and re-layouts  62.2 us
  transfers between devices with their start and end apart: 45, of which 19 were waited for; matrix products, arithmetic and copies ran while one was open for 12% of the time, Pallas kernels for 0%

profile of v1, /device:TPU:0, one launch (start us, length us, event | category | flops | bytes accessed | tf_op | source)
XLA Modules:
  0.0 711.7 jit_solution(7132212767002630932)
XLA Ops:
  0.0 5.0 collective-permute-start.39
  15.7 17.6 %collective-permute-done = f32[64,3072]{1,0:T(8,128)} collective-permute-done((f32[64,3072]{1,0:T(8,128)}, f32[64,3072]{1,0:T(8,128)}, u32[]{:S(2)}, u32[]{:S(2)}) %collective-permute-start) | collective-permute-done | bytes 786464 | tf_op jit(solution)/shard_map/ppermute | solution.py:48
  42.8 31.0 %collective-permute-done.40 = f32[64,3072]{1,0:T(8,128)} collective-permute-done((f32[64,3072]{1,0:T(8,128)}, f32[64,3072]{1,0:T(8,128)}, u32[]{:S(2)}, u32[]{:S(2)}) %collective-permute-start.40) | collective-permute-done | bytes 786464 | tf_op jit(solution)/shard_map/ppermute | solution.py:48
  84.9 3.6 fusion.95
  88.5 3.6 fusion.97
  92.3 66.0 %collective-permute-start.27 = (f32[256,512]{1,0:T(8,128)S(1)}, f32[256,512]{1,0:T(8,128)S(1)}, u32[]{:S(2)}, u32[]{:S(2)}) collective-permute-start(f32[256,512]{1,0:T(8,128)S(1)} %get-tuple-element.71), channel_id=1, source_target_pairs={{0,8},{2,10},{4,12},{6,14},{8,16},{10,18},{12,20},{14,22},{16,24},... | collective-permute-start | bytes 1572872 | tf_op jit(solution)/shard_map/ppermute | solution.py:48
  163.3 5.1 fusion.96
  172.1 70.1 %collective-permute-done.28 = f32[256,512]{1,0:T(8,128)S(1)} collective-permute-done((f32[256,512]{1,0:T(8,128)S(1)}, f32[256,512]{1,0:T(8,128)S(1)}, u32[]{:S(2)}, u32[]{:S(2)}) %collective-permute-start.28) | collective-permute-done | bytes 524320 | tf_op jit(solution)/shard_map/ppermute | solution.py:48
  247.4 24.5 %collective-permute-done.30 = f32[128,512]{1,0:T(8,128)S(1)} collective-permute-done((f32[128,512]{1,0:T(8,128)S(1)}, f32[128,512]{1,0:T(8,128)S(1)}, u32[]{:S(2)}, u32[]{:S(2)}) %collective-permute-start.30) | collective-permute-done | bytes 262176 | tf_op jit(solution)/shard_map/ppermute | solution.py:48
  273.9 4.4 collective-permute-done.31
  279.4 34.3 %collective-permute-start.18 = (f32[128,512]{1,0:T(8,128)S(1)}, f32[128,512]{1,0:T(8,128)S(1)}, u32[]{:S(2)}, u32[]{:S(2)}) collective-permute-start(f32[128,512]{1,0:T(8,128)S(1)} %get-tuple-element.98), channel_id=1, source_target_pairs={{0,8},{2,10},{4,12},{6,14},{8,16},{10,18},{12,20},{14,22},{16,24},... | collective-permute-start | bytes 786440 | tf_op jit(solution)/shard_map/ppermute | solution.py:48
  320.5 6.2 collective-permute-done.33
  327.3 4.3 collective-permute-done.20
  333.5 3.2 collective-permute-done.21
  338.9 13.7 %collective-permute-start.10 = (f32[64,512]{1,0:T(8,128)S(1)}, f32[64,512]{1,0:T(8,128)S(1)}, u32[]{:S(2)}, u32[]{:S(2)}) collective-permute-start(f32[64,512]{1,0:T(8,128)S(1)} %get-tuple-element.119), channel_id=1, source_target_pairs={{0,16},{2,18},{4,20},{6,22},{8,24},{10,26},{12,28},{14,30},{16,0},... | collective-permute-start | bytes 393224 | tf_op jit(solution)/shard_map/ppermute | solution.py:48
  352.6 4.7 collective-permute-start.11
  357.8 3.1 collective-permute-done.10
  364.5 3.3 collective-permute-start.12
  367.8 14.8 %collective-permute-start.13 = (f32[64,512]{1,0:T(8,128)S(1)}, f32[64,512]{1,0:T(8,128)S(1)}, u32[]{:S(2)}, u32[]{:S(2)}) collective-permute-start(f32[64,512]{1,0:T(8,128)S(1)} %get-tuple-element.12), channel_id=1, source_target_pairs={{0,16},{2,18},{4,20},{6,22},{8,24},{10,26},{12,28},{14,30},{16,0},... | collective-permute-start | bytes 393224 | tf_op jit(solution)/shard_map/ppermute | solution.py:48
  382.7 7.5 %collective-permute-done.35 = f32[256,512]{1,0:T(8,128)S(1)} collective-permute-done((f32[256,512]{1,0:T(8,128)S(1)}, f32[256,512]{1,0:T(8,128)S(1)}, u32[]{:S(2)}, u32[]{:S(2)}) %collective-permute-start.35) | collective-permute-done | bytes 524320 | tf_op jit(solution)/shard_map/ppermute | solution.py:48
  393.5 13.6 %collective-permute-done.13 = f32[64,512]{1,0:T(8,128)S(1)} collective-permute-done((f32[64,512]{1,0:T(8,128)S(1)}, f32[64,512]{1,0:T(8,128)S(1)}, u32[]{:S(2)}, u32[]{:S(2)}) %collective-permute-start.13) | collective-permute-done | bytes 131104 | tf_op jit(solution)/shard_map/ppermute | solution.py:48
  407.3 4.2 collective-permute-done.36
  411.4 9.9 %collective-permute-start.25 = (f32[128,512]{1,0:T(8,128)S(1)}, f32[128,512]{1,0:T(8,128)S(1)}, u32[]{:S(2)}, u32[]{:S(2)}) collective-permute-start(f32[128,512]{1,0:T(8,128)S(1)} %pad_maximum_fusion.6), channel_id=1, source_target_pairs={{0,8},{2,10},{4,12},{6,14},{8,16},{10,18},{12,20},{14,22},{16,24},... | collective-permute-start | bytes 786440 | tf_op jit(solution)/shard_map/ppermute | solution.py:48
  422.1 9.2 %collective-permute-done.24 = f32[128,512]{1,0:T(8,128)S(1)} collective-permute-done((f32[128,512]{1,0:T(8,128)S(1)}, f32[128,512]{1,0:T(8,128)S(1)}, u32[]{:S(2)}, u32[]{:S(2)}) %collective-permute-start.24) | collective-permute-done | bytes 262176 | tf_op jit(solution)/shard_map/ppermute | solution.py:48
  437.0 20.5 %collective-permute-done.26 = f32[512,512]{1,0:T(8,128)S(1)} collective-permute-done((f32[512,512]{1,0:T(8,128)S(1)}, f32[512,512]{1,0:T(8,128)S(1)}, u32[]{:S(2)}, u32[]{:S(2)}) %collective-permute-start.26) | collective-permute-done | bytes 1048608 | tf_op jit(solution)/shard_map/ppermute | solution.py:48
  457.7 3.7 fusion.104
  461.5 51.8 %collective-permute-done.16 = f32[512,512]{1,0:T(8,128)S(1)} collective-permute-done((f32[512,512]{1,0:T(8,128)S(1)}, f32[512,512]{1,0:T(8,128)S(1)}, u32[]{:S(2)}, u32[]{:S(2)}) %collective-permute-start.16) | collective-permute-done | bytes 1048608 | tf_op jit(solution)/shard_map/ppermute | solution.py:48
  513.5 3.7 fusion.107
  517.2 6.3 add_add_fusion.1
  541.8 48.9 %collective-permute-done.43 = f32[512,3072]{1,0:T(8,128)} collective-permute-done((f32[512,3072]{1,0:T(8,128)}, f32[512,3072]{1,0:T(8,128)}, u32[]{:S(2)}, u32[]{:S(2)}) %collective-permute-start.43) | collective-permute-done | bytes 6291488 | tf_op jit(solution)/shard_map/ppermute | solution.py:48
  615.4 27.7 %fusion.91 = f32[1024,3072]{1,0:T(8,128)} fusion(f32[1024,3072]{1,0:T(8,128)} %slice_dynamic-update-slice_fusion, f32[1024,1024]{1,0:T(8,128)S(1)} %get-tuple-element.6, f32[1024]{0:T(1024)S(1)} %bitcast.37, f32[1024]{0:T(1024)S(1)} %add_rsqrt_fusion, f32[1024]{0:T(1024)S(1)} %broadcast_multiply_fusion), kind=kOutput, calls=%fused_computation.128 | convolution fusion | flops 19330498560 | bytes 29372416 | tf_op jit(solution)/shard_map/dot_general | solution.py:11
  643.1 55.6 %fusion.278 = (f32[1024,1024]{1,0:T(8,128)}, f32[1024,1024]{1,0:T(8,128)S(1)}) fusion(f32[1024,1024]{1,0:T(8,128)S(1)} %get-tuple-element.6, f32[1024,3072]{1,0:T(8,128)} %slice_dynamic-update-slice_fusion.12, f32[1024,3072]{1,0:T(8,128)} %fusion.91, f32[3072]{0:T(1024)S(1)} %copy-done.6), kind=kOutput, calls=%fused_computation.553 | convolution fusion | flops 19532873728 | bytes 37761024 | tf_op jit(solution)/shard_map/dot_general | solution.py:11
  (269 shorter events, 128.0 us)
Async XLA Ops:
  0.0 39.6 %collective-permute-start.39 = (f32[64,3072]{1,0:T(8,128)}, f32[64,3072]{1,0:T(8,128)}, u32[]{:S(2)}, u32[]{:S(2)}) collective-permute-start(f32[64,3072]{1,0:T(8,128)} %param.15), channel_id=1, source_target_pairs={{0,24},{2,26},{4,28},{6,30},{8,0},{10,2},{12,4},{14,6},{16,8},{18,... | collective-permute-start | bytes 2359304 | tf_op jit(solution)/shard_map/ppermute | solution.py:48
  5.1 68.8 %collective-permute-start.40 = (f32[64,3072]{1,0:T(8,128)}, f32[64,3072]{1,0:T(8,128)}, u32[]{:S(2)}, u32[]{:S(2)}) collective-permute-start(f32[64,3072]{1,0:T(8,128)} %param.15), channel_id=1, source_target_pairs={{0,16},{2,18},{4,20},{6,22},{8,24},{10,26},{12,28},{14,30},{16,0},... | collective-permute-start | bytes 2359304 | tf_op jit(solution)/shard_map/ppermute | solution.py:48
  5.1 70.8 %collective-permute-start.41 = (f32[64,3072]{1,0:T(8,128)}, f32[64,3072]{1,0:T(8,128)S(1)}, u32[]{:S(2)}, u32[]{:S(2)}) collective-permute-start(f32[64,3072]{1,0:T(8,128)} %param.15), channel_id=1, source_target_pairs={{0,8},{2,10},{4,12},{6,14},{8,16},{10,18},{12,20},{14,22},{16,24},... | collective-permute-start | bytes 2359304 | tf_op jit(solution)/shard_map/ppermute | solution.py:48
  12.9 65.6 %collective-permute-start.5 = (f32[512,1024]{1,0:T(8,128)S(1)}, f32[512,1024]{1,0:T(8,128)}, u32[]{:S(2)}, u32[]{:S(2)}) collective-permute-start(f32[512,1024]{1,0:T(8,128)S(1)} %bitcast.15), channel_id=1, source_target_pairs={{0,1},{1,0},{2,3},{3,2},{4,5},{5,4},{6,7},{7,6},{8,9},{9,8},{10,11... | collective-permute-start | bytes 6291464 | tf_op jit(solution)/shard_map/ppermute | solution.py:51
  13.0 20.3 %collective-permute-start = (f32[64,3072]{1,0:T(8,128)}, f32[64,3072]{1,0:T(8,128)}, u32[]{:S(2)}, u32[]{:S(2)}) collective-permute-start(f32[64,3072]{1,0:T(8,128)} %bitcast.21), channel_id=1, source_target_pairs={{0,4},{2,6},{4,0},{6,2},{8,12},{10,14},{12,8},{14,10},{16,20},{18,... | collective-permute-start | bytes 2359304 | tf_op jit(solution)/shard_map/ppermute | solution.py:48
  34.8 133.9 %collective-permute-start.1 = (f32[128,3072]{1,0:T(8,128)S(1)}, f32[128,3072]{1,0:T(8,128)S(1)}, u32[]{:S(2)}, u32[]{:S(2)}) collective-permute-start(f32[128,3072]{1,0:T(8,128)S(1)} %pad_maximum_fusion.1), channel_id=1, source_target_pairs={{0,24},{2,26},{4,28},{6,30},{8,0},{10,2},{12,4},{14,6},{16,8},{18,... | collective-permute-start | bytes 4718600 | tf_op jit(solution)/shard_map/ppermute | solution.py:48
  39.6 205.9 %collective-permute-start.2 = (f32[128,3072]{1,0:T(8,128)S(1)}, f32[128,3072]{1,0:T(8,128)S(1)}, u32[]{:S(2)}, u32[]{:S(2)}) collective-permute-start(f32[128,3072]{1,0:T(8,128)S(1)} %pad_maximum_fusion.1), channel_id=1, source_target_pairs={{0,16},{2,18},{4,20},{6,22},{8,24},{10,26},{12,28},{14,30},{16,0},... | collective-permute-start | bytes 4718600 | tf_op jit(solution)/shard_map/ppermute | solution.py:48
  92.3 78.4 %collective-permute-start.27 = (f32[256,512]{1,0:T(8,128)S(1)}, f32[256,512]{1,0:T(8,128)S(1)}, u32[]{:S(2)}, u32[]{:S(2)}) collective-permute-start(f32[256,512]{1,0:T(8,128)S(1)} %get-tuple-element.71), channel_id=1, source_target_pairs={{0,8},{2,10},{4,12},{6,14},{8,16},{10,18},{12,20},{14,22},{16,24},... | collective-permute-start | bytes 1572872 | tf_op jit(solution)/shard_map/ppermute | solution.py:48
  158.3 84.0 %collective-permute-start.28 = (f32[256,512]{1,0:T(8,128)S(1)}, f32[256,512]{1,0:T(8,128)S(1)}, u32[]{:S(2)}, u32[]{:S(2)}) collective-permute-start(f32[256,512]{1,0:T(8,128)S(1)} %get-tuple-element.73), channel_id=1, source_target_pairs={{0,16},{2,18},{4,20},{6,22},{8,24},{10,26},{12,28},{14,30},{16,0},... | collective-permute-start | bytes 1572872 | tf_op jit(solution)/shard_map/ppermute | solution.py:48
  160.1 83.6 %collective-permute-start.29 = (f32[256,512]{1,0:T(8,128)S(1)}, f32[256,512]{1,0:T(8,128)S(1)}, u32[]{:S(2)}, u32[]{:S(2)}) collective-permute-start(f32[256,512]{1,0:T(8,128)S(1)} %get-tuple-element.72), channel_id=1, source_target_pairs={{0,24},{2,26},{4,28},{6,30},{8,0},{10,2},{12,4},{14,6},{16,8},{18,... | collective-permute-start | bytes 1572872 | tf_op jit(solution)/shard_map/ppermute | solution.py:48
  168.8 103.8 %collective-permute-start.3 = (f32[128,3072]{1,0:T(8,128)S(1)}, f32[128,3072]{1,0:T(8,128)S(1)}, u32[]{:S(2)}, u32[]{:S(2)}) collective-permute-start(f32[128,3072]{1,0:T(8,128)S(1)} %pad_maximum_fusion.1), channel_id=1, source_target_pairs={{0,8},{2,10},{4,12},{6,14},{8,16},{10,18},{12,20},{14,22},{16,24},... | collective-permute-start | bytes 4718600 | tf_op jit(solution)/shard_map/ppermute | solution.py:48
  170.6 261.3 %collective-permute-start.42 = (f32[256,3072]{1,0:T(8,128)S(1)}, f32[256,3072]{1,0:T(8,128)S(1)}, u32[]{:S(2)}, u32[]{:S(2)}) collective-permute-start(f32[256,3072]{1,0:T(8,128)S(1)} %pad_maximum_fusion), channel_id=1, source_target_pairs={{0,2},{2,0},{4,6},{6,4},{8,10},{10,8},{12,14},{14,12},{16,18},{18,... | collective-permute-start | bytes 9437192 | tf_op jit(solution)/shard_map/ppermute | solution.py:48
  242.2 36.9 %collective-permute-start.17 = (f32[512,512]{1,0:T(8,128)S(1)}, f32[512,512]{1,0:T(8,128)S(1)}, u32[]{:S(2)}, u32[]{:S(2)}) collective-permute-start(f32[512,512]{1,0:T(8,128)S(1)} %pad_maximum_fusion.2), channel_id=1, source_target_pairs={{0,4},{2,6},{4,0},{6,2},{8,12},{10,14},{12,8},{14,10},{16,20},{18,... | collective-permute-start | bytes 3145736 | tf_op jit(solution)/shard_map/ppermute | solution.py:48
  243.8 72.0 %collective-permute-start.7 = (f32[512,512]{1,0:T(8,128)S(1)}, f32[512,512]{1,0:T(8,128)S(1)}, u32[]{:S(2)}, u32[]{:S(2)}) collective-permute-start(f32[512,512]{1,0:T(8,128)S(1)} %get-tuple-element.82), channel_id=1, source_target_pairs={{0,2},{2,0},{4,6},{6,4},{8,10},{10,8},{12,14},{14,12},{16,18},{18,... | collective-permute-start | bytes 3145736 | tf_op jit(solution)/shard_map/ppermute | solution.py:48
  245.6 26.4 %collective-permute-start.30 = (f32[128,512]{1,0:T(8,128)S(1)}, f32[128,512]{1,0:T(8,128)S(1)}, u32[]{:S(2)}, u32[]{:S(2)}) collective-permute-start(f32[128,512]{1,0:T(8,128)S(1)} %pad_maximum_fusion.7), channel_id=1, source_target_pairs={{0,2},{2,0},{4,6},{6,4},{8,10},{10,8},{12,14},{14,12},{16,18},{18,... | collective-permute-start | bytes 786440 | tf_op jit(solution)/shard_map/ppermute | solution.py:48
  278.6 40.2 %collective-permute-start.32 = (f32[64,512]{1,0:T(8,128)S(1)}, f32[64,512]{1,0:T(8,128)S(1)}, u32[]{:S(2)}, u32[]{:S(2)}) collective-permute-start(f32[64,512]{1,0:T(8,128)S(1)} %get-tuple-element.8), channel_id=1, source_target_pairs={{0,4},{2,6},{4,0},{6,2},{8,12},{10,14},{12,8},{14,10},{16,20},{18,... | collective-permute-start | bytes 393224 | tf_op jit(solution)/shard_map/ppermute | solution.py:48
  279.4 47.8 %collective-permute-start.18 = (f32[128,512]{1,0:T(8,128)S(1)}, f32[128,512]{1,0:T(8,128)S(1)}, u32[]{:S(2)}, u32[]{:S(2)}) collective-permute-start(f32[128,512]{1,0:T(8,128)S(1)} %get-tuple-element.98), channel_id=1, source_target_pairs={{0,8},{2,10},{4,12},{6,14},{8,16},{10,18},{12,20},{14,22},{16,24},... | collective-permute-start | bytes 786440 | tf_op jit(solution)/shard_map/ppermute | solution.py:48
  315.7 15.8 %collective-permute-start.20 = (f32[128,512]{1,0:T(8,128)S(1)}, f32[128,512]{1,0:T(8,128)S(1)}, u32[]{:S(2)}, u32[]{:S(2)}) collective-permute-start(f32[128,512]{1,0:T(8,128)S(1)} %get-tuple-element.99), channel_id=1, source_target_pairs={{0,24},{2,26},{4,28},{6,30},{8,0},{10,2},{12,4},{14,6},{16,8},{18,... | collective-permute-start | bytes 786440 | tf_op jit(solution)/shard_map/ppermute | solution.py:48
  327.2 40.6 %collective-permute-start.34 = (f32[256,512]{1,0:T(8,128)S(1)}, f32[256,512]{1,0:T(8,128)S(1)}, u32[]{:S(2)}, u32[]{:S(2)}) collective-permute-start(f32[256,512]{1,0:T(8,128)S(1)} %pad_maximum_fusion.5), channel_id=1, source_target_pairs={{0,24},{2,26},{4,28},{6,30},{8,0},{10,2},{12,4},{14,6},{16,8},{18,... | collective-permute-start | bytes 1572872 | tf_op jit(solution)/shard_map/ppermute | solution.py:48
  337.0 20.2 %collective-permute-start.22 = (f32[64,512]{1,0:T(8,128)S(1)}, f32[64,512]{1,0:T(8,128)S(1)}, u32[]{:S(2)}, u32[]{:S(2)}) collective-permute-start(f32[64,512]{1,0:T(8,128)S(1)} %get-tuple-element.10), channel_id=1, source_target_pairs={{0,2},{2,0},{4,6},{6,4},{8,10},{10,8},{12,14},{14,12},{16,18},{18,... | collective-permute-start | bytes 393224 | tf_op jit(solution)/shard_map/ppermute | solution.py:48
  338.9 22.0 %collective-permute-start.10 = (f32[64,512]{1,0:T(8,128)S(1)}, f32[64,512]{1,0:T(8,128)S(1)}, u32[]{:S(2)}, u32[]{:S(2)}) collective-permute-start(f32[64,512]{1,0:T(8,128)S(1)} %get-tuple-element.119), channel_id=1, source_target_pairs={{0,16},{2,18},{4,20},{6,22},{8,24},{10,26},{12,28},{14,30},{16,0},... | collective-permute-start | bytes 393224 | tf_op jit(solution)/shard_map/ppermute | solution.py:48
  360.9 162.9 %collective-permute-start.4 = (f32[512,3072]{1,0:T(8,128)}, f32[512,3072]{1,0:T(8,128)S(1)}, u32[]{:S(2)}, u32[]{:S(2)}) collective-permute-start(f32[512,3072]{1,0:T(8,128)} %constant_dynamic-update-slice_fusion), channel_id=1, source_target_pairs={{0,2},{2,0},{4,6},{6,4},{8,10},{10,8},{12,14},{14,12},{16,18},{18,... | collective-permute-start | bytes 18874376 | tf_op jit(solution)/shard_map/ppermute | solution.py:48
  361.0 29.1 %collective-permute-start.35 = (f32[256,512]{1,0:T(8,128)S(1)}, f32[256,512]{1,0:T(8,128)S(1)}, u32[]{:S(2)}, u32[]{:S(2)}) collective-permute-start(f32[256,512]{1,0:T(8,128)S(1)} %pad_maximum_fusion.5), channel_id=1, source_target_pairs={{0,16},{2,18},{4,20},{6,22},{8,24},{10,26},{12,28},{14,30},{16,0},... | collective-permute-start | bytes 1572872 | tf_op jit(solution)/shard_map/ppermute | solution.py:48
  364.5 28.4 %collective-permute-start.12 = (f32[64,512]{1,0:T(8,128)S(1)}, f32[64,512]{1,0:T(8,128)S(1)}, u32[]{:S(2)}, u32[]{:S(2)}) collective-permute-start(f32[64,512]{1,0:T(8,128)S(1)} %get-tuple-element.12), channel_id=1, source_target_pairs={{0,24},{2,26},{4,28},{6,30},{8,0},{10,2},{12,4},{14,6},{16,8},{18,... | collective-permute-start | bytes 393224 | tf_op jit(solution)/shard_map/ppermute | solution.py:48
  367.8 39.4 %collective-permute-start.13 = (f32[64,512]{1,0:T(8,128)S(1)}, f32[64,512]{1,0:T(8,128)S(1)}, u32[]{:S(2)}, u32[]{:S(2)}) collective-permute-start(f32[64,512]{1,0:T(8,128)S(1)} %get-tuple-element.12), channel_id=1, source_target_pairs={{0,16},{2,18},{4,20},{6,22},{8,24},{10,26},{12,28},{14,30},{16,0},... | collective-permute-start | bytes 393224 | tf_op jit(solution)/shard_map/ppermute | solution.py:48
  390.1 17.0 %collective-permute-start.14 = (f32[64,512]{1,0:T(8,128)S(1)}, f32[64,512]{1,0:T(8,128)S(1)}, u32[]{:S(2)}, u32[]{:S(2)}) collective-permute-start(f32[64,512]{1,0:T(8,128)S(1)} %get-tuple-element.12), channel_id=1, source_target_pairs={{0,8},{2,10},{4,12},{6,14},{8,16},{10,18},{12,20},{14,22},{16,24},... | collective-permute-start | bytes 393224 | tf_op jit(solution)/shard_map/ppermute | solution.py:48
  392.9 18.5 %collective-permute-start.36 = (f32[256,512]{1,0:T(8,128)S(1)}, f32[256,512]{1,0:T(8,128)S(1)}, u32[]{:S(2)}, u32[]{:S(2)}) collective-permute-start(f32[256,512]{1,0:T(8,128)S(1)} %pad_maximum_fusion.5), channel_id=1, source_target_pairs={{0,8},{2,10},{4,12},{6,14},{8,16},{10,18},{12,20},{14,22},{16,24},... | collective-permute-start | bytes 1572872 | tf_op jit(solution)/shard_map/ppermute | solution.py:48
  407.2 24.1 %collective-permute-start.24 = (f32[128,512]{1,0:T(8,128)S(1)}, f32[128,512]{1,0:T(8,128)S(1)}, u32[]{:S(2)}, u32[]{:S(2)}) collective-permute-start(f32[128,512]{1,0:T(8,128)S(1)} %pad_maximum_fusion.6), channel_id=1, source_target_pairs={{0,16},{2,18},{4,20},{6,22},{8,24},{10,26},{12,28},{14,30},{16,0},... | collective-permute-start | bytes 786440 | tf_op jit(solution)/shard_map/ppermute | solution.py:48
  411.4 19.9 %collective-permute-start.25 = (f32[128,512]{1,0:T(8,128)S(1)}, f32[128,512]{1,0:T(8,128)S(1)}, u32[]{:S(2)}, u32[]{:S(2)}) collective-permute-start(f32[128,512]{1,0:T(8,128)S(1)} %pad_maximum_fusion.6), channel_id=1, source_target_pairs={{0,8},{2,10},{4,12},{6,14},{8,16},{10,18},{12,20},{14,22},{16,24},... | collective-permute-start | bytes 786440 | tf_op jit(solution)/shard_map/ppermute | solution.py:48
  431.4 26.2 %collective-permute-start.26 = (f32[512,512]{1,0:T(8,128)S(1)}, f32[512,512]{1,0:T(8,128)S(1)}, u32[]{:S(2)}, u32[]{:S(2)}) collective-permute-start(f32[512,512]{1,0:T(8,128)S(1)} %constant_dynamic-update-slice_fusion.60), channel_id=1, source_target_pairs={{0,4},{2,6},{4,0},{6,2},{8,12},{10,14},{12,8},{14,10},{16,20},{18,... | collective-permute-start | bytes 3145736 | tf_op jit(solution)/shard_map/ppermute | solution.py:48
  433.8 156.9 %collective-permute-start.43 = (f32[512,3072]{1,0:T(8,128)}, f32[512,3072]{1,0:T(8,128)}, u32[]{:S(2)}, u32[]{:S(2)}) collective-permute-start(f32[512,3072]{1,0:T(8,128)} %constant_dynamic-update-slice_fusion.90), channel_id=1, source_target_pairs={{0,4},{2,6},{4,0},{6,2},{8,12},{10,14},{12,8},{14,10},{16,20},{18,... | collective-permute-start | bytes 18874376 | tf_op jit(solution)/shard_map/ppermute | solution.py:48
  436.3 76.9 %collective-permute-start.16 = (f32[512,512]{1,0:T(8,128)S(1)}, f32[512,512]{1,0:T(8,128)S(1)}, u32[]{:S(2)}, u32[]{:S(2)}) collective-permute-start(f32[512,512]{1,0:T(8,128)S(1)} %constant_dynamic-update-slice_fusion.39), channel_id=1, source_target_pairs={{0,2},{2,0},{4,6},{6,4},{8,10},{10,8},{12,14},{14,12},{16,18},{18,... | collective-permute-start | bytes 3145736 | tf_op jit(solution)/shard_map/ppermute | solution.py:48
  (24 other events, 317.3 us)

commit v2 on v0

v2 whole, which is shorter than its diff:
```python
import functools

import jax
import jax.numpy as jnp
from jax import lax
from jax.experimental import pallas as pl
from jax.experimental.pallas import tpu as pltpu
from jax.sharding import PartitionSpec as P

epsilon = 1e-05
exact = lax.Precision.HIGH
grant = 40 * 1024 * 1024


def contract(left, right):
    return lax.dot_general(
        left, right, (((1,), (1,)), ((), ())), precision=exact, preferred_element_type=jnp.float32
    )


def together(*values):
    return lax.optimization_barrier(values)


def halves(value):
    high = value.astype(jnp.bfloat16)
    return high, (value - high.astype(jnp.float32)).astype(jnp.bfloat16)


def three_pass(left, right):
    def product(a, b):
        return jnp.dot(a, b, preferred_element_type=jnp.float32)

    return product(left[0], right[0]) + (product(left[0], right[1]) + product(left[1], right[0]))


def column_norm(values, gain):
    centre = jnp.mean(values, axis=0, keepdims=True)
    centred = values - centre
    spread = jnp.mean(centred * centred, axis=0, keepdims=True)
    return centred * lax.rsqrt(spread + epsilon) * gain


def tile_of(size):
    return 256 if size % 256 == 0 else size


def norm_two_kernel(count, fields_ref, gain_ref, *refs):
    terms, (mixed_ref, high_ref, low_ref) = refs[:-3], refs[-3:]
    parts = []
    for piece in range(count):
        own = terms[piece :: count]
        total = own[0][...]
        for ref in own[1:]:
            total = total + ref[...]
        parts.append(total)
    mixed = fields_ref[...] + jnp.concatenate(parts, axis=0)
    mixed_ref[...] = mixed
    high_ref[...], low_ref[...] = halves(column_norm(mixed, gain_ref[...]))


def norm_two(fields, gain, terms, count):
    rows, width = fields.shape
    tile = tile_of(width)
    whole = pl.BlockSpec((rows, tile), lambda n: (0, n))
    piece = pl.BlockSpec((rows // count, tile), lambda n: (0, n))
    return pl.pallas_call(
        functools.partial(norm_two_kernel, count),
        grid=(width // tile,),
        in_specs=[whole, pl.BlockSpec((rows, 1), lambda n: (0, 0))] + [piece] * len(terms),
        out_specs=[whole] * 3,
        out_shape=[jax.ShapeDtypeStruct((rows, width), kind) for kind in (jnp.float32, jnp.bfloat16, jnp.bfloat16)],
        compiler_params=pltpu.CompilerParams(vmem_limit_bytes=grant),
        cost_estimate=pl.CostEstimate(
            flops=12 * rows * width, bytes_accessed=4 * rows * width * (4 + len(terms) // count), transcendentals=0
        ),
        name="norm_two",
    )(fields, gain, *terms)


def expand_kernel(count, high_ref, low_ref, bias_ref, *refs):
    pieces, (out_high, out_low, weight_high, weight_low) = refs[:count], refs[count:]
    depth = pieces[0].shape[0]

    @pl.when(pl.program_id(0) == 0)
    def _():
        for n, piece in enumerate(pieces):
            columns = slice(n * depth, (n + 1) * depth)
            weight_high[:, columns], weight_low[:, columns] = halves(piece[...].T)

    total = three_pass((weight_high[...], weight_low[...]), (high_ref[...], low_ref[...])) + bias_ref[...]
    active = 0.5 * total * (1.0 + lax.erf(total * 0.7071067811865476))
    out_high[...], out_low[...] = halves(active)


def expand(high, low, bias, pieces):
    depth, width = high.shape
    units = pieces[0].shape[1]
    tile = tile_of(width)
    normed = pl.BlockSpec((depth, tile), lambda n: (0, n))
    return pl.pallas_call(
        functools.partial(expand_kernel, len(pieces)),
        grid=(width // tile,),
        in_specs=[normed, normed, pl.BlockSpec((units, 1), lambda n: (0, 0))]
        + [pl.BlockSpec(piece.shape, lambda n: (0, 0)) for piece in pieces],
        out_specs=[pl.BlockSpec((units, tile), lambda n: (0, n))] * 2,
        out_shape=[jax.ShapeDtypeStruct((units, width), jnp.bfloat16)] * 2,
        scratch_shapes=[pltpu.VMEM((units, depth), jnp.bfloat16)] * 2,
        compiler_params=pltpu.CompilerParams(vmem_limit_bytes=grant),
        cost_estimate=pl.CostEstimate(
            flops=6 * units * depth * width,
            bytes_accessed=4 * (units * depth + depth * width + units * width),
            transcendentals=units * width,
        ),
        name="expand",
    )(high, low, bias, *pieces)


def reduce_kernel(places, first, high_ref, low_ref, *refs):
    count = len(places)
    pieces, refs = refs[:count], refs[count:]
    if not first:
        start_ref, refs = refs[0], refs[1:]
    out_ref, weight_high, weight_low = refs

    @pl.when(pl.program_id(0) == 0)
    def _():
        for piece, starts in zip(pieces, places):
            rows = piece.shape[0] // len(starts)
            for n, start in enumerate(starts):
                high, low = halves(piece[n * rows : (n + 1) * rows, :])
                weight_high[start : start + rows, :] = high
                weight_low[start : start + rows, :] = low

    total = three_pass((weight_high[...], weight_low[...]), (high_ref[...], low_ref[...]))
    out_ref[...] = total if first else start_ref[...] + total


def reduce(high, low, pieces, places, start):
    units, width = high.shape
    rows = sum(piece.shape[0] for piece in pieces)
    tile = tile_of(width)
    hidden = pl.BlockSpec((units, tile), lambda n: (0, n))
    total = pl.BlockSpec((rows, tile), lambda n: (0, n))
    first = start is None
    return pl.pallas_call(
        functools.partial(reduce_kernel, places, first),
        grid=(width // tile,),
        in_specs=[hidden, hidden]
        + [pl.BlockSpec(piece.shape, lambda n: (0, 0)) for piece in pieces]
        + ([] if first else [total]),
        out_specs=total,
        out_shape=jax.ShapeDtypeStruct((rows, width), jnp.float32),
        scratch_shapes=[pltpu.VMEM((rows, units), jnp.bfloat16)] * 2,
        compiler_params=pltpu.CompilerParams(vmem_limit_bytes=grant),
        cost_estimate=pl.CostEstimate(
            flops=6 * units * rows * width,
            bytes_accessed=4 * (units * rows + 2 * rows * width + units * width),
            transcendentals=0,
        ),
        name="reduce",
    )(high, low, *pieces, *([] if first else [start]))


class Grid:
    def __init__(self, tok, ch):
        self.tok, self.ch, self.deep = tok, ch, tok // 4
        self.pieces = [(b, a) for b in range(2) for a in range(2)]
        self.keys = [(c, b, a) for b, a in self.pieces for c in range(self.deep)]

    def index(self, z, y, x):
        return (z * 2 + y) * 2 + x

    def place(self, chip):
        return chip // 4, chip // 2 % 2, chip % 2

    def move(self, value, dz=0, dy=0, dx=0):
        pairs = []
        for chip in range(self.tok):
            z, y, x = self.place(chip)
            pairs.append((chip, self.index((z + dz) % self.deep, (y + dy) % 2, (x + dx) % 2)))
        return lax.ppermute(value, "tok", pairs)

    def to_core(self, value, step):
        return lax.ppermute(value, "ch", [(core, (core + step) % self.ch) for core in range(self.ch)])

    def along_z(self, value):
        return [value] + [self.move(value, dz=-step) for step in range(1, self.deep)]


def shards(
    grid,
    fields,
    gain_one,
    tok_in_weight,
    tok_in_bias,
    tok_out_weight,
    gain_two,
    ch_in_weight,
    ch_in_bias,
    ch_out_weight,
):
    ch, deep = grid.ch, grid.deep
    width = fields.shape[1]
    rows = ch * width // grid.tok
    per_core = width // rows
    core = lax.axis_index("ch")
    z, y, x = grid.place(lax.axis_index("tok"))
    owners = [grid.index((z + c) % deep, (y + b) % 2, (x + a) % 2) for c, b, a in grid.keys]
    cut = lambda value, n: value[n * (value.shape[0] // 2) : (n + 1) * (value.shape[0] // 2)]

    def all_cores(value):
        return jnp.concatenate([value] + [grid.to_core(value, ch - step) for step in range(1, ch)], axis=0)

    def by_offset(value):
        starts = [(((owner // per_core - core) % ch) * per_core + owner % per_core) * rows for owner in owners]
        return jnp.concatenate([lax.dynamic_slice_in_dim(value, start, rows, 0) for start in starts], axis=0)

    def for_core(value, step):
        taken = []
        for n in range(per_core):
            oz, oy, ox = grid.place(((core + step) % ch) * per_core + n)
            start = ((((oy - y) % 2) * 2 + (ox - x) % 2) * deep + (oz - z) % deep) * rows
            taken.append(lax.dynamic_slice_in_dim(value, start, rows, 0))
        return jnp.concatenate(taken, axis=0)

    units = ch_in_weight.shape[1]
    ends = [units * n // 3 for n in range(4)]
    spans = list(zip(ends, ends[1:]))
    out_rows = ch_out_weight.T
    in_bias = ch_in_bias[:, None]
    second_own = [out_rows[:, a:b] for a, b in spans]

    full = all_cores(fields.T)
    gains = by_offset(all_cores(gain_one[:, None])), by_offset(all_cores(gain_two[:, None]))
    first_z = grid.along_z(ch_in_weight)
    last_y = grid.move(second_own[2], dy=1)
    full = by_offset(full)
    normed = column_norm(full, gains[0])
    normed, last_y = together(normed, last_y)
    last_pair = jnp.concatenate([second_own[2], last_y], axis=0)
    last_x = grid.move(last_pair, dx=1)

    quarter = normed.shape[0] // 4
    piece = [normed[n * quarter : (n + 1) * quarter] for n in range(4)]
    middle = tok_in_weight.shape[0] // 2
    weight_a, weight_b = tok_in_weight[:middle], tok_in_weight[middle:]
    sent_a = grid.move(contract(jnp.concatenate([piece[1], piece[3]], axis=0), weight_a), dx=1)
    sent_b = grid.move(contract(cut(normed, 1), weight_b), dy=1)
    kept_a = contract(jnp.concatenate([piece[0], piece[2]], axis=0), weight_a)
    kept_b = contract(cut(normed, 0), weight_b)

    sent_a, sent_b, last_x = together(sent_a, sent_b, last_x)
    part_a, part_b = kept_a + sent_a, kept_b + sent_b
    sent_a, sent_b = grid.move(cut(part_a, 1), dy=1), grid.move(cut(part_b, 1), dx=1)
    sent_a, sent_b, *first_z = together(sent_a, sent_b, *first_z)
    partial = jnp.concatenate([cut(part_a, 0) + sent_a, cut(part_b, 0) + sent_b], axis=1)
    sent = [grid.move(partial[step * rows : (step + 1) * rows], dz=step) for step in range(1, deep)]
    line = [jnp.concatenate([value[:, a:b] for value in first_z], axis=0) for a, b in spans]
    first_x = [grid.move(line[n], dx=1) for n in range(2)]
    first_y = {2: grid.move(line[2], dy=1)}

    *sent, first_x[0] = together(*sent, first_x[0])
    summed = partial[:rows]
    for value in sent:
        summed = summed + value
    activated = jax.nn.gelu(summed + tok_in_bias[None, :], approximate=False)
    active_z = grid.along_z(activated)
    first_xy = {0: (grid.move(line[0], dy=1), grid.move(first_x[0], dy=1))}

    *active_z, second_z = together(*active_z, jnp.concatenate(second_own[:2], axis=1))
    active = jnp.concatenate(active_z, axis=0)
    active_a, active_b = active[:, :middle], active[:, middle:]
    second_z = grid.along_z(second_z)
    step_a, step_b = grid.move(active_a, dy=1), grid.move(active_b, dx=1)
    step_a, step_b = together(step_a, step_b)
    all_a = [active_a, grid.move(active_a, dx=1), step_a, grid.move(step_a, dx=1)]
    all_b = [active_b, step_b, grid.move(active_b, dy=1), grid.move(step_b, dy=1)]
    fenced = together(all_a[1], all_a[3], all_b[2], all_b[3], *second_z, *first_xy[0], first_x[1], first_y[2], last_x)
    all_a[1], all_a[3], all_b[2], all_b[3] = fenced[:4]
    second_z = fenced[4 : 4 + deep]
    first_xy[0] = fenced[4 + deep : 6 + deep]
    first_x[1], first_y[2], last_x = fenced[6 + deep :]

    first_xy[1] = grid.move(line[1], dy=1), grid.move(first_x[1], dy=1)
    first_xy[2] = grid.move(line[2], dx=1), grid.move(first_y[2], dx=1)
    last_block = jnp.concatenate([last_pair, last_x], axis=0)
    last_z = grid.along_z(last_block)
    size = spans[0][1]
    line_two = [jnp.concatenate([v[:, :size] for v in second_z], axis=0), jnp.concatenate([v[:, size:] for v in second_z], axis=0)]

    terms = [
        contract(a, tok_out_weight[:, :middle]) + contract(b, tok_out_weight[:, middle:])
        for a, b in zip(all_a, all_b)
    ]
    arrived = [grid.to_core(value, step) for step in range(1, ch) for value in terms]
    mixed, high, low = norm_two(full, gains[1], terms + arrived, 4)

    biases = [in_bias[a:b] for a, b in spans]
    hidden = {0: expand(high, low, biases[0], [line[0], first_x[0], *first_xy[0]])}
    *first_xy[1], line_two[0] = together(*first_xy[1], line_two[0])
    *first_xy[2], line_two[1] = together(*first_xy[2], line_two[1])
    second_y = grid.move(line_two[0], dy=1)
    second_x = grid.move(line_two[1], dx=1)
    hidden[1] = expand(high, low, biases[1], [line[1], first_x[1], *first_xy[1]])
    hidden[2] = expand(high, low, biases[2], [line[2], first_xy[2][0], first_y[2], first_xy[2][1]])
    second_yx = grid.move(line_two[0], dx=1), grid.move(second_y, dx=1)
    second_xy = grid.move(line_two[1], dy=1), grid.move(second_x, dy=1)

    block = rows * deep
    plain = [[n * block] for n in range(4)]
    across = [[((b * 2 + a) * deep + c) * rows for a in range(2) for b in range(2)] for c in range(deep)]
    total = reduce(*hidden[2], last_z, across, None)
    total = reduce(*hidden[0], [line_two[0], second_yx[0], second_y, second_yx[1]], plain, total)
    total = reduce(*hidden[1], [line_two[1], second_x, *second_xy], plain, total)

    result = for_core(total + mixed, 0)
    for step in range(1, ch):
        result = result + grid.to_core(for_core(total, step), step)
    return result.T


def solution(mesh):
    grid = Grid(mesh.shape["tok"], mesh.shape["ch"])
    in_specs = (
        P("tok", "ch"),
        P("ch"),
        P("ch", "tok"),
        P("ch"),
        P("tok", "ch"),
        P("ch"),
        P("tok", "ch"),
        P("ch"),
        P("ch", "tok"),
    )

    def block(*arrays):
        return shards(grid, *arrays)

    return jax.shard_map(block, mesh=mesh, in_specs=in_specs, out_specs=P("tok", "ch"), check_vma=False)
```

time: 757 us -> 510 us (0.67); the launches traced: 757 us -> 501 us
  waiting for transfers between devices: 545 us -> 282 us
  matrix products: 173 us -> 30.9 us
  Pallas kernels: 0 us -> 71.6 us
  starting transfers between devices: 0.25 us -> 58.5 us
  local copies, waits for them, and re-layouts: 6.64 us -> 37.4 us
  between operations: 13.5 us -> 2.32 us
    all_gather x4 -> x0, waiting for transfers between devices: 362 us -> none  [the longest x1 149 us: shards(): lax.all_gather(ch_in_weight, 'tok', axis=0, tiled=True)]
    ppermute x0 -> x50, waiting for transfers between devices: none -> 282 us  [the longest x42 282 us: move(): return lax.ppermute(value, 'tok', pairs)]
    reduce_scatter x2 -> x0, waiting for transfers between devices: 157 us -> none  [the longest x1 147 us: shards(): lax.psum_scatter(lax.dot_general(columns, tok_in_weight, (((0,), (1,)), (...]
    dot_general x4 -> x12, matrix products: 173 us -> 30.9 us  [contract(): lax.dot_general(left, right, (((1,), (1,)), ((), ())), precision=exact, p...]
    pallas_call x0 -> x7, Pallas kernels: none -> 71.6 us  [the longest x3 34.6 us: expand(): pl.pallas_call(functools.partial(expand_kernel, len(pieces)), grid=(width...]
    ppermute x0 -> x50, starting transfers between devices: none -> 58.5 us  [the longest x42 56.8 us: move(): return lax.ppermute(value, 'tok', pairs)]
    psum x1 -> x0, waiting for transfers between devices: 23.7 us -> none  [shards(): mixed_sum = lax.psum(partial_value, 'ch')]
    unnamed x9 -> x108, local copies, waits for them, and re-layouts: 4.83 us -> 24.4 us
  transfers between devices with their start and end apart: 7 -> 50, of which waited for: 7 -> 19; matrix products, arithmetic and copies ran while one was open for 7% -> 10% of each run, Pallas kernels for 0% -> 12%
where the time goes in v2:
time: 510 us; the launch traced here: 501 us
  waiting for transfers between devices  282 us (55%)
  Pallas kernels  71.6 us (14%)
  starting transfers between devices  58.5 us (11%)
  local copies, waits for them, and re-layouts  37.4 us (7%)
  matrix products  30.9 us (6%)
  other arithmetic  17.8 us (3%)
    ppermute x42, waiting for transfers between devices, move(): return lax.ppermute(value, 'tok', pairs)  282 us
    ppermute x42, starting transfers between devices, move(): return lax.ppermute(value, 'tok', pairs)  56.8 us
    pallas_call x3, Pallas kernels, expand(): pl.pallas_call(functools.partial(expand_kernel, len(pieces)), grid=(width...  34.6 us
    pallas_call x3, Pallas kernels, reduce(): pl.pallas_call(functools.partial(reduce_kernel, places, first), grid=(wid...  31.1 us
    dot_general x12, matrix products, contract(): lax.dot_general(left, right, (((1,), (1,)), ((), ())), precision=exact, p...  30.9 us
    unnamed x108, local copies, waits for them, and re-layouts  24.4 us
  transfers between devices with their start and end apart: 50, of which 19 were waited for; matrix products, arithmetic and copies ran while one was open for 10% of the time, Pallas kernels for 12%

profile of v2, /device:TPU:0, one launch (start us, length us, event | category | flops | bytes accessed | tf_op | source)
XLA Modules:
  0.0 500.7 jit_solution(6844796684661654549)
XLA Ops:
  19.5 2.8 fusion.4
  27.6 3.6 collective-permute-start.9
  31.2 39.5 %collective-permute-done.6 = f32[128,1024]{1,0:T(8,128)} collective-permute-done((f32[128,1024]{1,0:T(8,128)S(1)}, f32[128,1024]{1,0:T(8,128)}, u32[]{:S(2)}, u32[]{:S(2)}) %collective-permute-start.6) | collective-permute-done | bytes 524320 | tf_op jit(solution)/shard_map/ppermute | solution.py:182
  73.0 2.8 fusion.37
  77.5 2.8 fusion.32
  81.8 16.3 %collective-permute-done.10 = f32[64,3072]{1,0:T(8,128)S(1)} collective-permute-done((f32[64,3072]{1,0:T(8,128)S(1)}, f32[64,3072]{1,0:T(8,128)S(1)}, u32[]{:S(2)}, u32[]{:S(2)}) %collective-permute-start.10) | collective-permute-done | bytes 786464 | tf_op jit(solution)/shard_map/ppermute | solution.py:182
  106.6 8.5 %collective-permute-done.12 = f32[64,1536]{1,0:T(8,128)S(1)} collective-permute-done((f32[64,1536]{1,0:T(8,128)S(1)}, f32[64,1536]{1,0:T(8,128)S(1)}, u32[]{:S(2)}, u32[]{:S(2)}) %collective-permute-start.12) | collective-permute-done | bytes 393248 | tf_op jit(solution)/shard_map/ppermute | solution.py:182
  115.1 15.0 %collective-permute-done.13 = f32[64,1536]{1,0:T(8,128)S(1)} collective-permute-done((f32[64,1536]{1,0:T(8,128)S(1)}, f32[64,1536]{1,0:T(8,128)S(1)}, u32[]{:S(2)}, u32[]{:S(2)}) %collective-permute-start.13) | collective-permute-done | bytes 393248 | tf_op jit(solution)/shard_map/ppermute | solution.py:182
  131.1 9.3 %collective-permute-start.16 = (f32[64,1536]{1,0:T(8,128)S(1)}, f32[64,1536]{1,0:T(8,128)S(1)}, u32[]{:S(2)}, u32[]{:S(2)}) collective-permute-start(f32[64,1536]{1,0:T(8,128)S(1)} %fusion.55), channel_id=1, source_target_pairs={{0,24},{2,26},{4,28},{6,30},{8,0},{10,2},{12,4},{14,6},{16,8},{18,... | collective-permute-start | bytes 1179656 | tf_op jit(solution)/shard_map/ppermute | solution.py:182
  142.8 7.2 %collective-permute-done.16 = f32[64,1536]{1,0:T(8,128)S(1)} collective-permute-done((f32[64,1536]{1,0:T(8,128)S(1)}, f32[64,1536]{1,0:T(8,128)S(1)}, u32[]{:S(2)}, u32[]{:S(2)}) %collective-permute-start.16) | collective-permute-done | bytes 393248 | tf_op jit(solution)/shard_map/ppermute | solution.py:182
  150.0 25.8 %collective-permute-done.17 = f32[64,1536]{1,0:T(8,128)S(1)} collective-permute-done((f32[64,1536]{1,0:T(8,128)S(1)}, f32[64,1536]{1,0:T(8,128)S(1)}, u32[]{:S(2)}, u32[]{:S(2)}) %collective-permute-start.17) | collective-permute-done | bytes 393248 | tf_op jit(solution)/shard_map/ppermute | solution.py:182
  186.1 13.1 %collective-permute-done.20 = f32[256,768]{1,0:T(8,128)} collective-permute-done((f32[256,768]{1,0:T(8,128)}, f32[256,768]{1,0:T(8,128)}, u32[]{:S(2)}, u32[]{:S(2)}) %collective-permute-start.20) | collective-permute-done | bytes 786464 | tf_op jit(solution)/shard_map/ppermute | solution.py:182
  200.7 19.4 %collective-permute-done.30.refs_1_ = f32[256,1024]{1,0:T(8,128)} collective-permute-done((f32[256,1024]{1,0:T(8,128)}, f32[256,1024]{1,0:T(8,128)}, u32[]{:S(2)}, u32[]{:S(2)}) %collective-permute-start.30) | collective-permute-done | bytes 1048608 | tf_op jit(solution)/shard_map/ppermute | solution.py:182
  222.6 9.3 %collective-permute-done.26 = f32[64,2048]{1,0:T(8,128)} collective-permute-done((f32[64,2048]{1,0:T(8,128)}, f32[64,2048]{1,0:T(8,128)}, u32[]{:S(2)}, u32[]{:S(2)}) %collective-permute-start.26) | collective-permute-done | bytes 524320 | tf_op jit(solution)/shard_map/ppermute | solution.py:182
  233.5 3.8 fusion.14
  237.2 3.5 fusion.42.refs_0_
  240.8 3.6 fusion.12
  249.4 13.8 %collective-permute-done.23 = f32[256,768]{1,0:T(8,128)S(1)} collective-permute-done((f32[256,768]{1,0:T(8,128)}, f32[256,768]{1,0:T(8,128)S(1)}, u32[]{:S(2)}, u32[]{:S(2)}) %collective-permute-start.23) | collective-permute-done | bytes 786464 | tf_op jit(solution)/shard_map/ppermute | solution.py:182
  263.2 16.8 %collective-permute-done.24 = f32[256,768]{1,0:T(8,128)S(1)} collective-permute-done((f32[256,768]{1,0:T(8,128)}, f32[256,768]{1,0:T(8,128)S(1)}, u32[]{:S(2)}, u32[]{:S(2)}) %collective-permute-start.24) | collective-permute-done | bytes 786464 | tf_op jit(solution)/shard_map/ppermute | solution.py:182
  291.8 10.7 %collective-permute-done.36.refs_2_ = f32[256,1024]{1,0:T(8,128)S(1)} collective-permute-done((f32[256,1024]{1,0:T(8,128)}, f32[256,1024]{1,0:T(8,128)S(1)}, u32[]{:S(2)}, u32[]{:S(2)}) %collective-permute-start.36) | collective-permute-done | bytes 1048608 | tf_op jit(solution)/shard_map/ppermute | solution.py:182
  305.0 16.9 %collective-permute-done.37.refs_3_ = f32[256,1024]{1,0:T(8,128)S(1)} collective-permute-done((f32[256,1024]{1,0:T(8,128)}, f32[256,1024]{1,0:T(8,128)S(1)}, u32[]{:S(2)}, u32[]{:S(2)}) %collective-permute-start.37) | collective-permute-done | bytes 1048608 | tf_op jit(solution)/shard_map/ppermute | solution.py:182
  327.2 17.1 %collective-permute-done.39.refs_3_ = f32[256,1024]{1,0:T(8,128)S(1)} collective-permute-done((f32[256,1024]{1,0:T(8,128)}, f32[256,1024]{1,0:T(8,128)S(1)}, u32[]{:S(2)}, u32[]{:S(2)}) %collective-permute-start.39) | collective-permute-done | bytes 1048608 | tf_op jit(solution)/shard_map/ppermute | solution.py:182
  351.3 5.9 %norm_two.1 = (f32[1024,1024]{1,0:T(8,128)}, bf16[1024,1024]{1,0:T(8,128)(2,1)S(1)}, bf16[1024,1024]{1,0:T(8,128)(2,1)S(1)}) custom-call(f32[1024,1024]{1,0:T(8,128)} %copy-done.25, f32[1024,1]{1,0:T(8,128)S(1)} %copy.20.gain_ref, f32[256,1024]{1,0:T(8,128)S(1)} %fusion.42.refs_0_, f32[256,1024]{1,0:T(8,128)S(1)} %fusion.45.refs_1_, ...), custom_call_target="tpu_custom_call" | custom-call | flops 12582912 | bytes 25165824 | tf_op jit(solution)/shard_map/norm_two/pallas_call | solution.py:67
  359.7 11.6 %expand.3 = (bf16[1024,1024]{1,0:T(8,128)(2,1)S(1)}, bf16[1024,1024]{1,0:T(8,128)(2,1)S(1)}) custom-call(bf16[1024,1024]{1,0:T(8,128)(2,1)S(1)} %get-tuple-element.81.high_ref, bf16[1024,1024]{1,0:T(8,128)(2,1)S(1)} %get-tuple-element.82.low_ref, f32[1024,1]{1,0:T(8,128)S(1)} %copy-done.2, f32[256,1024]{1,0:T(8,128)} %pad_maximum_fusion.1.refs_0_, ...), custom_call_target="tpu_custom_call" | custom-call | flops 6442450944 | bytes 12582912 | tf_op jit(solution)/shard_map/expand/pallas_call | solution.py:101
  372.6 11.9 %expand.4 = (bf16[1024,1024]{1,0:T(8,128)(2,1)S(1)}, bf16[1024,1024]{1,0:T(8,128)(2,1)S(1)}) custom-call(bf16[1024,1024]{1,0:T(8,128)(2,1)S(1)} %get-tuple-element.81.high_ref, bf16[1024,1024]{1,0:T(8,128)(2,1)S(1)} %get-tuple-element.82.low_ref, f32[1024,1]{1,0:T(8,128)S(1)} %copy-done.1, f32[256,1024]{1,0:T(8,128)S(1)} %pad_maximum_fusion.refs_0_, ...), custom_call_target="tpu_custom_call" | custom-call | flops 6442450944 | bytes 12582912 | tf_op jit(solution)/shard_map/expand/pallas_call | solution.py:101
  389.3 11.1 %expand.5 = (bf16[1024,1024]{1,0:T(8,128)(2,1)S(1)}, bf16[1024,1024]{1,0:T(8,128)(2,1)S(1)}) custom-call(bf16[1024,1024]{1,0:T(8,128)(2,1)S(1)} %get-tuple-element.81.high_ref, bf16[1024,1024]{1,0:T(8,128)(2,1)S(1)} %get-tuple-element.82.low_ref, f32[1024,1]{1,0:T(8,128)S(1)} %copy.23.bias_ref, f32[256,1024]{1,0:T(8,128)S(1)} %pad_maximum_fusion.2.refs_0_, ...), custom_call_target="tpu_custom_call" | custom-call | flops 6442450944 | bytes 12582912 | tf_op jit(solution)/shard_map/expand/pallas_call | solution.py:101
  400.4 34.5 %collective-permute-done.47.refs_2_ = f32[256,1024]{1,0:T(8,128)} collective-permute-done((f32[256,1024]{1,0:T(8,128)S(1)}, f32[256,1024]{1,0:T(8,128)}, u32[]{:S(2)}, u32[]{:S(2)}) %collective-permute-start.47) | collective-permute-done | bytes 1048608 | tf_op jit(solution)/shard_map/ppermute | solution.py:182
  437.0 10.5 %reduce.19.refs_4_ = f32[1024,1024]{1,0:T(8,128)S(1)} custom-call(bf16[1024,1024]{1,0:T(8,128)(2,1)S(1)} %get-tuple-element.101.high_ref, bf16[1024,1024]{1,0:T(8,128)(2,1)S(1)} %get-tuple-element.102.low_ref, f32[256,1024]{1,0:T(8,128)S(1)} %pad_maximum_fusion.5.refs_0_, f32[256,1024]{1,0:T(8,128)} %collective-permute-done.46.refs_1_, ...), custom_call_target="tpu_custom_call" | custom-call | flops 6442450944 | bytes 16777216 | tf_op jit(solution)/shard_map/reduce/pallas_call | solution.py:146
  451.1 10.5 %reduce.20.refs_4_ = f32[1024,1024]{1,0:T(8,128)S(1)} custom-call(bf16[1024,1024]{1,0:T(8,128)(2,1)S(1)} %copy-done.22, bf16[1024,1024]{1,0:T(8,128)(2,1)S(1)} %copy-done.24, f32[256,1024]{1,0:T(8,128)S(1)} %pad_maximum_fusion.3.refs_0_, f32[256,1024]{1,0:T(8,128)S(1)} %collective-permute-done.43.refs_1_, f32[256,1024]{1,0:T(8,128)} %collective-permute-done.44.refs_2_, ...), custom_call_target="tpu_custom_call" | custom-call | flops 6442450944 | bytes 16777216 | tf_op jit(solution)/shard_map/reduce/pallas_call | solution.py:146
  463.6 15.1 %collective-permute-done.42.refs_3_ = f32[256,1024]{1,0:T(8,128)S(1)} collective-permute-done((f32[256,1024]{1,0:T(8,128)}, f32[256,1024]{1,0:T(8,128)S(1)}, u32[]{:S(2)}, u32[]{:S(2)}) %collective-permute-start.42) | collective-permute-done | bytes 1048608 | tf_op jit(solution)/shard_map/ppermute | solution.py:182
  478.7 10.1 %reduce.21 = f32[1024,1024]{1,0:T(8,128)S(1)} custom-call(bf16[1024,1024]{1,0:T(8,128)(2,1)S(1)} %copy-done.18, bf16[1024,1024]{1,0:T(8,128)(2,1)S(1)} %copy-done.20, f32[256,1024]{1,0:T(8,128)S(1)} %pad_maximum_fusion.4.refs_0_, f32[256,1024]{1,0:T(8,128)} %collective-permute-done.40.refs_1_, f32[256,1024]{1,0:T(8,128)S(1)} %collective-permute-done.41.refs_2_, ...), custom_call_target="tpu_custom_call" | custom-call | flops 6442450944 | bytes 16777216 | tf_op jit(solution)/shard_map/reduce/pallas_call | solution.py:146
  491.8 4.4 add.1191
  (254 shorter events, 111.3 us)
Async XLA Ops:
  22.3 50.8 %collective-permute-start.4 = (f32[512,768]{1,0:T(8,128)S(1)}, f32[512,768]{1,0:T(8,128)S(1)}, u32[]{:S(2)}, u32[]{:S(2)}) collective-permute-start(f32[512,768]{1,0:T(8,128)S(1)} %fusion.4), channel_id=1, source_target_pairs={{0,2},{2,0},{4,6},{6,4},{8,10},{10,8},{12,14},{14,12},{16,18},{18,... | collective-permute-start | bytes 4718600 | tf_op jit(solution)/shard_map/ppermute | solution.py:182
  24.5 48.6 %collective-permute-start.5 = (f32[512,768]{1,0:T(8,128)S(1)}, f32[512,768]{1,0:T(8,128)S(1)}, u32[]{:S(2)}, u32[]{:S(2)}) collective-permute-start(f32[512,768]{1,0:T(8,128)S(1)} %fusion.2), channel_id=1, source_target_pairs={{0,4},{2,6},{4,0},{6,2},{8,12},{10,14},{12,8},{14,10},{16,20},{18,... | collective-permute-start | bytes 4718600 | tf_op jit(solution)/shard_map/ppermute | solution.py:182
  27.0 43.7 %collective-permute-start.6 = (f32[128,1024]{1,0:T(8,128)S(1)}, f32[128,1024]{1,0:T(8,128)}, u32[]{:S(2)}, u32[]{:S(2)}) collective-permute-start(f32[128,1024]{1,0:T(8,128)S(1)} %pad_maximum_fusion.6), channel_id=1, source_target_pairs={{0,2},{2,0},{4,6},{6,4},{8,10},{10,8},{12,14},{14,12},{16,18},{18,... | collective-permute-start | bytes 1572872 | tf_op jit(solution)/shard_map/ppermute | solution.py:182
  27.6 54.2 %collective-permute-start.9 = (f32[64,3072]{1,0:T(8,128)S(1)}, f32[64,3072]{1,0:T(8,128)S(1)}, u32[]{:S(2)}, u32[]{:S(2)}) collective-permute-start(f32[64,3072]{1,0:T(8,128)S(1)} %copy-done.28), channel_id=1, source_target_pairs={{0,24},{2,26},{4,28},{6,30},{8,0},{10,2},{12,4},{14,6},{16,8},{18,... | collective-permute-start | bytes 2359304 | tf_op jit(solution)/shard_map/ppermute | solution.py:182
  31.2 66.9 %collective-permute-start.10 = (f32[64,3072]{1,0:T(8,128)S(1)}, f32[64,3072]{1,0:T(8,128)S(1)}, u32[]{:S(2)}, u32[]{:S(2)}) collective-permute-start(f32[64,3072]{1,0:T(8,128)S(1)} %copy-done.28), channel_id=1, source_target_pairs={{0,16},{2,18},{4,20},{6,22},{8,24},{10,26},{12,28},{14,30},{16,0},... | collective-permute-start | bytes 2359304 | tf_op jit(solution)/shard_map/ppermute | solution.py:182
  99.2 31.0 %collective-permute-start.15 = (f32[256,1024]{1,0:T(8,128)S(1)}, f32[256,1024]{1,0:T(8,128)S(1)}, u32[]{:S(2)}, u32[]{:S(2)}) collective-permute-start(f32[256,1024]{1,0:T(8,128)S(1)} %pad_maximum_fusion.refs_0_), channel_id=1, source_target_pairs={{0,2},{2,0},{4,6},{6,4},{8,10},{10,8},{12,14},{14,12},{16,18},{18,... | collective-permute-start | bytes 3145736 | tf_op jit(solution)/shard_map/ppermute | solution.py:182
  140.4 35.4 %collective-permute-start.17 = (f32[64,1536]{1,0:T(8,128)S(1)}, f32[64,1536]{1,0:T(8,128)S(1)}, u32[]{:S(2)}, u32[]{:S(2)}) collective-permute-start(f32[64,1536]{1,0:T(8,128)S(1)} %fusion.55), channel_id=1, source_target_pairs={{0,16},{2,18},{4,20},{6,22},{8,24},{10,26},{12,28},{14,30},{16,0},... | collective-permute-start | bytes 1179656 | tf_op jit(solution)/shard_map/ppermute | solution.py:182
  141.5 34.3 %collective-permute-start.18 = (f32[64,1536]{1,0:T(8,128)S(1)}, f32[64,1536]{1,0:T(8,128)S(1)}, u32[]{:S(2)}, u32[]{:S(2)}) collective-permute-start(f32[64,1536]{1,0:T(8,128)S(1)} %fusion.55), channel_id=1, source_target_pairs={{0,8},{2,10},{4,12},{6,14},{8,16},{10,18},{12,20},{14,22},{16,24},... | collective-permute-start | bytes 1179656 | tf_op jit(solution)/shard_map/ppermute | solution.py:182
  142.3 43.7 %collective-permute-start.28 = (f32[256,1024]{1,0:T(8,128)S(1)}, f32[256,1024]{1,0:T(8,128)}, u32[]{:S(2)}, u32[]{:S(2)}) collective-permute-start(f32[256,1024]{1,0:T(8,128)S(1)} %pad_maximum_fusion.refs_0_), channel_id=1, source_target_pairs={{0,4},{2,6},{4,0},{6,2},{8,12},{10,14},{12,8},{14,10},{16,20},{18,... | collective-permute-start | bytes 3145736 | tf_op jit(solution)/shard_map/ppermute | solution.py:182
  180.5 39.6 %collective-permute-start.30 = (f32[256,1024]{1,0:T(8,128)}, f32[256,1024]{1,0:T(8,128)}, u32[]{:S(2)}, u32[]{:S(2)}) collective-permute-start(f32[256,1024]{1,0:T(8,128)} %pad_maximum_fusion.1.refs_0_), channel_id=1, source_target_pairs={{0,2},{2,0},{4,6},{6,4},{8,10},{10,8},{12,14},{14,12},{16,18},{18,... | collective-permute-start | bytes 3145736 | tf_op jit(solution)/shard_map/ppermute | solution.py:182
  182.1 39.5 %collective-permute-start.31 = (f32[256,1024]{1,0:T(8,128)S(1)}, f32[256,1024]{1,0:T(8,128)}, u32[]{:S(2)}, u32[]{:S(2)}) collective-permute-start(f32[256,1024]{1,0:T(8,128)S(1)} %pad_maximum_fusion.2.refs_0_), channel_id=1, source_target_pairs={{0,4},{2,6},{4,0},{6,2},{8,12},{10,14},{12,8},{14,10},{16,20},{18,... | collective-permute-start | bytes 3145736 | tf_op jit(solution)/shard_map/ppermute | solution.py:182
  186.0 36.1 %collective-permute-start.25 = (f32[64,2048]{1,0:T(8,128)}, f32[64,2048]{1,0:T(8,128)}, u32[]{:S(2)}, u32[]{:S(2)}) collective-permute-start(f32[64,2048]{1,0:T(8,128)} %concatenate.81), channel_id=1, source_target_pairs={{0,24},{2,26},{4,28},{6,30},{8,0},{10,2},{12,4},{14,6},{16,8},{18,... | collective-permute-start | bytes 1572872 | tf_op jit(solution)/shard_map/ppermute | solution.py:182
  199.2 32.7 %collective-permute-start.26 = (f32[64,2048]{1,0:T(8,128)}, f32[64,2048]{1,0:T(8,128)}, u32[]{:S(2)}, u32[]{:S(2)}) collective-permute-start(f32[64,2048]{1,0:T(8,128)} %concatenate.81), channel_id=1, source_target_pairs={{0,16},{2,18},{4,20},{6,22},{8,24},{10,26},{12,28},{14,30},{16,0},... | collective-permute-start | bytes 1572872 | tf_op jit(solution)/shard_map/ppermute | solution.py:182
  199.7 32.7 %collective-permute-start.27 = (f32[64,2048]{1,0:T(8,128)}, f32[64,2048]{1,0:T(8,128)}, u32[]{:S(2)}, u32[]{:S(2)}) collective-permute-start(f32[64,2048]{1,0:T(8,128)} %concatenate.81), channel_id=1, source_target_pairs={{0,8},{2,10},{4,12},{6,14},{8,16},{10,18},{12,20},{14,22},{16,24},... | collective-permute-start | bytes 1572872 | tf_op jit(solution)/shard_map/ppermute | solution.py:182
  222.1 41.1 %collective-permute-start.23 = (f32[256,768]{1,0:T(8,128)}, f32[256,768]{1,0:T(8,128)S(1)}, u32[]{:S(2)}, u32[]{:S(2)}) collective-permute-start(f32[256,768]{1,0:T(8,128)} %get-tuple-element.167), channel_id=1, source_target_pairs={{0,4},{2,6},{4,0},{6,2},{8,12},{10,14},{12,8},{14,10},{16,20},{18,... | collective-permute-start | bytes 2359304 | tf_op jit(solution)/shard_map/ppermute | solution.py:182
  231.8 31.3 %collective-permute-start.22 = (f32[256,768]{1,0:T(8,128)}, f32[256,768]{1,0:T(8,128)S(1)}, u32[]{:S(2)}, u32[]{:S(2)}) collective-permute-start(f32[256,768]{1,0:T(8,128)} %collective-permute-done.20), channel_id=1, source_target_pairs={{0,2},{2,0},{4,6},{6,4},{8,10},{10,8},{12,14},{14,12},{16,18},{18,... | collective-permute-start | bytes 2359304 | tf_op jit(solution)/shard_map/ppermute | solution.py:182
  232.4 47.6 %collective-permute-start.24 = (f32[256,768]{1,0:T(8,128)}, f32[256,768]{1,0:T(8,128)S(1)}, u32[]{:S(2)}, u32[]{:S(2)}) collective-permute-start(f32[256,768]{1,0:T(8,128)} %collective-permute-done.21), channel_id=1, source_target_pairs={{0,4},{2,6},{4,0},{6,2},{8,12},{10,14},{12,8},{14,10},{16,20},{18,... | collective-permute-start | bytes 2359304 | tf_op jit(solution)/shard_map/ppermute | solution.py:182
  247.3 55.2 %collective-permute-start.36 = (f32[256,1024]{1,0:T(8,128)}, f32[256,1024]{1,0:T(8,128)S(1)}, u32[]{:S(2)}, u32[]{:S(2)}) collective-permute-start(f32[256,1024]{1,0:T(8,128)} %pad_maximum_fusion.1.refs_0_), channel_id=1, source_target_pairs={{0,4},{2,6},{4,0},{6,2},{8,12},{10,14},{12,8},{14,10},{16,20},{18,... | collective-permute-start | bytes 3145736 | tf_op jit(solution)/shard_map/ppermute | solution.py:182
  248.8 54.6 %collective-permute-start.38 = (f32[256,1024]{1,0:T(8,128)S(1)}, f32[256,1024]{1,0:T(8,128)S(1)}, u32[]{:S(2)}, u32[]{:S(2)}) collective-permute-start(f32[256,1024]{1,0:T(8,128)S(1)} %pad_maximum_fusion.2.refs_0_), channel_id=1, source_target_pairs={{0,2},{2,0},{4,6},{6,4},{8,10},{10,8},{12,14},{14,12},{16,18},{18,... | collective-permute-start | bytes 3145736 | tf_op jit(solution)/shard_map/ppermute | solution.py:182
  263.2 82.1 %collective-permute-start.32 = (f32[256,1024]{1,0:T(8,128)S(1)}, f32[256,1024]{1,0:T(8,128)S(1)}, u32[]{:S(2)}, u32[]{:S(2)}) collective-permute-start(f32[256,1024]{1,0:T(8,128)S(1)} %fusion.42.refs_0_), channel_id=1, source_target_pairs={{0,1},{1,0},{2,3},{3,2},{4,5},{5,4},{6,7},{7,6},{8,9},{9,8},{10,11... | collective-permute-start | bytes 3145736 | tf_op jit(solution)/shard_map/ppermute | solution.py:185
  281.6 40.3 %collective-permute-start.37 = (f32[256,1024]{1,0:T(8,128)}, f32[256,1024]{1,0:T(8,128)S(1)}, u32[]{:S(2)}, u32[]{:S(2)}) collective-permute-start(f32[256,1024]{1,0:T(8,128)} %collective-permute-done.30.refs_1_), channel_id=1, source_target_pairs={{0,4},{2,6},{4,0},{6,2},{8,12},{10,14},{12,8},{14,10},{16,20},{18,... | collective-permute-start | bytes 3145736 | tf_op jit(solution)/shard_map/ppermute | solution.py:182
  286.2 60.9 %collective-permute-start.33 = (f32[256,1024]{1,0:T(8,128)S(1)}, f32[256,1024]{1,0:T(8,128)S(1)}, u32[]{:S(2)}, u32[]{:S(2)}) collective-permute-start(f32[256,1024]{1,0:T(8,128)S(1)} %fusion.45.refs_1_), channel_id=1, source_target_pairs={{0,1},{1,0},{2,3},{3,2},{4,5},{5,4},{6,7},{7,6},{8,9},{9,8},{10,11... | collective-permute-start | bytes 3145736 | tf_op jit(solution)/shard_map/ppermute | solution.py:185
  303.5 45.7 %collective-permute-start.34 = (f32[256,1024]{1,0:T(8,128)S(1)}, f32[256,1024]{1,0:T(8,128)S(1)}, u32[]{:S(2)}, u32[]{:S(2)}) collective-permute-start(f32[256,1024]{1,0:T(8,128)S(1)} %fusion.48.refs_2_), channel_id=1, source_target_pairs={{0,1},{1,0},{2,3},{3,2},{4,5},{5,4},{6,7},{7,6},{8,9},{9,8},{10,11... | collective-permute-start | bytes 3145736 | tf_op jit(solution)/shard_map/ppermute | solution.py:185
  304.5 45.3 %collective-permute-start.35 = (f32[256,1024]{1,0:T(8,128)S(1)}, f32[256,1024]{1,0:T(8,128)S(1)}, u32[]{:S(2)}, u32[]{:S(2)}) collective-permute-start(f32[256,1024]{1,0:T(8,128)S(1)} %fusion.51.refs_3_), channel_id=1, source_target_pairs={{0,1},{1,0},{2,3},{3,2},{4,5},{5,4},{6,7},{7,6},{8,9},{9,8},{10,11... | collective-permute-start | bytes 3145736 | tf_op jit(solution)/shard_map/ppermute | solution.py:185
  345.2 42.0 %collective-permute-start.46 = (f32[256,1024]{1,0:T(8,128)S(1)}, f32[256,1024]{1,0:T(8,128)}, u32[]{:S(2)}, u32[]{:S(2)}) collective-permute-start(f32[256,1024]{1,0:T(8,128)S(1)} %pad_maximum_fusion.5.refs_0_), channel_id=1, source_target_pairs={{0,24},{2,26},{4,28},{6,30},{8,0},{10,2},{12,4},{14,6},{16,8},{18,... | collective-permute-start | bytes 3145736 | tf_op jit(solution)/shard_map/ppermute | solution.py:182
  345.2 89.7 %collective-permute-start.47 = (f32[256,1024]{1,0:T(8,128)S(1)}, f32[256,1024]{1,0:T(8,128)}, u32[]{:S(2)}, u32[]{:S(2)}) collective-permute-start(f32[256,1024]{1,0:T(8,128)S(1)} %pad_maximum_fusion.5.refs_0_), channel_id=1, source_target_pairs={{0,16},{2,18},{4,20},{6,22},{8,24},{10,26},{12,28},{14,30},{16,0},... | collective-permute-start | bytes 3145736 | tf_op jit(solution)/shard_map/ppermute | solution.py:182
  347.2 89.8 %collective-permute-start.48 = (f32[256,1024]{1,0:T(8,128)S(1)}, f32[256,1024]{1,0:T(8,128)}, u32[]{:S(2)}, u32[]{:S(2)}) collective-permute-start(f32[256,1024]{1,0:T(8,128)S(1)} %pad_maximum_fusion.5.refs_0_), channel_id=1, source_target_pairs={{0,8},{2,10},{4,12},{6,14},{8,16},{10,18},{12,20},{14,22},{16,24},... | collective-permute-start | bytes 3145736 | tf_op jit(solution)/shard_map/ppermute | solution.py:182
  349.2 87.3 %collective-permute-start.40 = (f32[256,1024]{1,0:T(8,128)S(1)}, f32[256,1024]{1,0:T(8,128)}, u32[]{:S(2)}, u32[]{:S(2)}) collective-permute-start(f32[256,1024]{1,0:T(8,128)S(1)} %pad_maximum_fusion.4.refs_0_), channel_id=1, source_target_pairs={{0,2},{2,0},{4,6},{6,4},{8,10},{10,8},{12,14},{14,12},{16,18},{18,... | collective-permute-start | bytes 3145736 | tf_op jit(solution)/shard_map/ppermute | solution.py:182
  349.8 38.9 %collective-permute-start.44 = (f32[256,1024]{1,0:T(8,128)S(1)}, f32[256,1024]{1,0:T(8,128)}, u32[]{:S(2)}, u32[]{:S(2)}) collective-permute-start(f32[256,1024]{1,0:T(8,128)S(1)} %pad_maximum_fusion.3.refs_0_), channel_id=1, source_target_pairs={{0,4},{2,6},{4,0},{6,2},{8,12},{10,14},{12,8},{14,10},{16,20},{18,... | collective-permute-start | bytes 3145736 | tf_op jit(solution)/shard_map/ppermute | solution.py:182
  387.3 62.2 %collective-permute-start.43 = (f32[256,1024]{1,0:T(8,128)S(1)}, f32[256,1024]{1,0:T(8,128)S(1)}, u32[]{:S(2)}, u32[]{:S(2)}) collective-permute-start(f32[256,1024]{1,0:T(8,128)S(1)} %pad_maximum_fusion.3.refs_0_), channel_id=1, source_target_pairs={{0,2},{2,0},{4,6},{6,4},{8,10},{10,8},{12,14},{14,12},{16,18},{18,... | collective-permute-start | bytes 3145736 | tf_op jit(solution)/shard_map/ppermute | solution.py:182
  388.7 60.8 %collective-permute-start.45 = (f32[256,1024]{1,0:T(8,128)}, f32[256,1024]{1,0:T(8,128)S(1)}, u32[]{:S(2)}, u32[]{:S(2)}) collective-permute-start(f32[256,1024]{1,0:T(8,128)} %collective-permute-done.44.refs_2_), channel_id=1, source_target_pairs={{0,2},{2,0},{4,6},{6,4},{8,10},{10,8},{12,14},{14,12},{16,18},{18,... | collective-permute-start | bytes 3145736 | tf_op jit(solution)/shard_map/ppermute | solution.py:182
  436.4 42.3 %collective-permute-start.42 = (f32[256,1024]{1,0:T(8,128)}, f32[256,1024]{1,0:T(8,128)S(1)}, u32[]{:S(2)}, u32[]{:S(2)}) collective-permute-start(f32[256,1024]{1,0:T(8,128)} %collective-permute-done.40.refs_1_), channel_id=1, source_target_pairs={{0,4},{2,6},{4,0},{6,2},{8,12},{10,14},{12,8},{14,10},{16,20},{18,... | collective-permute-start | bytes 3145736 | tf_op jit(solution)/shard_map/ppermute | solution.py:182
  (56 other events, 805.9 us)
